TPU v7x, 32 devices: a whole 2x2x4 slice. The times are simulated.
32 devices in a mesh: rows: 8 (over z, core), cols: 4 (over y, x).
Axes of the slice: x: 2, y: 2, z: 4, core: 2. Of those that a mesh axis runs over, the one named last changes fastest.
Arguments:
- source_points: float32 [32, 16384], P(None, ('rows', 'cols')), may hold values from -3.5 to 3.5
- target_points: float32 [32, 8192], P(None, ('cols', 'rows')), may hold values from -3.5 to 3.5
- target_init: float32 [8192], P('cols'), may hold values from -3 to 3
Outputs:
- source_potential: float32 [16384], P('rows')
- target_potential: float32 [8192], P('cols')
All inputs are finite; a program needn't handle non-finite values.
Results may differ from a plain program's by a relative error of at most 0.0003.
Values sent between devices are 32-bit elements; how exact they have to be, the bound alone decides.
No kernel may reach another device: no remote copies, remote signals or barrier semaphores. Data moves between devices by JAX's collectives and lax.ppermute only.
A program may use at most 64 MiB of HBM per device.

v0:
```python
import math

import jax
import jax.numpy as jnp
from jax import lax
from jax.sharding import PartitionSpec as P

ITERS = 4


eps = 0.2


def cost_block(left, right, sq_left, sq_right):
    cross = lax.dot_general(
        left,
        right,
        (((0,), (0,)), ((), ())),
        precision=lax.Precision.HIGHEST,
        preferred_element_type=jnp.float32,
    )
    return sq_left[:, None] + sq_right[None, :] - 2.0 * cross


def split_blocks(points, width):
    return points.reshape(points.shape[0], points.shape[1] // width, width).transpose(1, 0, 2)


def row_partials(src_blocks, sq_blocks, targets, sq_targets, potential_g):

    def row_one_block(items):
        block, sq_block = items
        scores = (potential_g[None, :] - cost_block(block, targets, sq_block, sq_targets)) / eps
        peak = jnp.max(scores, axis=1)
        return (peak, jnp.sum(jnp.exp(scores - peak[:, None]), axis=1))

    peak, total = lax.map(row_one_block, (src_blocks, sq_blocks))
    return (peak.reshape(-1), total.reshape(-1))


def col_partials(sources, sq_sources, tgt_blocks, sq_blocks, potential_f):

    def col_one_block(items):
        block, sq_block = items
        scores = (potential_f[:, None] - cost_block(sources, block, sq_sources, sq_block)) / eps
        peak = jnp.max(scores, axis=0)
        return (peak, jnp.sum(jnp.exp(scores - peak[None, :]), axis=0))

    peak, total = lax.map(col_one_block, (tgt_blocks, sq_blocks))
    return (peak.reshape(-1), total.reshape(-1))


def finish_rows(peak, total, ntgt):
    whole_peak = lax.pmax(peak, "cols")
    whole_total = lax.psum(total * jnp.exp(peak - whole_peak), "cols")
    return eps * math.log(ntgt) - eps * (whole_peak + jnp.log(whole_total))


def finish_cols(peak, total, nsrc):
    whole_peak = lax.pmax(peak, "rows")
    whole_total = lax.psum(total * jnp.exp(peak - whole_peak), "rows")
    return eps * math.log(nsrc) - eps * (whole_peak + jnp.log(whole_total))


def body(source_points, target_points, target_init):
    sources = lax.all_gather(source_points, "cols", axis=1, tiled=True)
    targets = lax.all_gather(target_points, "rows", axis=1, tiled=True)
    nsrc = sources.shape[1] * lax.axis_size("rows")
    ntgt = targets.shape[1] * lax.axis_size("cols")
    sq_sources = jnp.sum(sources * sources, axis=0)
    sq_targets = jnp.sum(targets * targets, axis=0)
    width_src = min(128, sources.shape[1])
    width_tgt = min(128, targets.shape[1])
    src_blocks = split_blocks(sources, width_src)
    tgt_blocks = split_blocks(targets, width_tgt)
    sq_src_blocks = sq_sources.reshape(-1, width_src)
    sq_tgt_blocks = sq_targets.reshape(-1, width_tgt)
    potential_g = target_init
    potential_f = jnp.zeros((sources.shape[1],), jnp.float32)
    for step in range(ITERS):
        peak, total = row_partials(src_blocks, sq_src_blocks, targets, sq_targets, potential_g)
        potential_f = finish_rows(peak, total, ntgt)
        peak, total = col_partials(sources, sq_sources, tgt_blocks, sq_tgt_blocks, potential_f)
        potential_g = finish_cols(peak, total, nsrc)
    return (potential_f, potential_g)


def solution(mesh):
    in_specs = (P(None, ("rows", "cols")), P(None, ("cols", "rows")), P("cols"))
    out_specs = (P("rows"), P("cols"))
    return jax.shard_map(body, mesh=mesh, in_specs=in_specs, out_specs=out_specs, check_vma=False)
```

profile of v0, /device:TPU:0, one launch (start us, length us, event | category | flops | bytes accessed | tf_op | source)
XLA Modules:
  0.0 425.9 jit_solution(15808384586652591447)
XLA Ops:
  0.6 10.7 %all_gather.6 = f32[32,2048]{1,0:T(8,128)S(1)} all-gather(f32[32,512]{1,0:T(8,128)} %param.19), channel_id=1, replica_groups=mesh['rows'=8,'cols'=4] {'cols'}, dimensions={1}, use_global_device_ids=true | all-gather | bytes 327680 | tf_op jit(solution)/shard_map/all_gather | solution.py:66
  12.1 14.4 %all_gather.7 = f32[32,2048]{1,0:T(8,128)S(1)} all-gather(f32[32,256]{1,0:T(8,128)S(1)} %copy-done), channel_id=1, replica_groups=mesh['rows'=8,'cols'=4] {'rows'}, dimensions={1}, use_global_device_ids=true | all-gather | bytes 294912 | tf_op jit(solution)/shard_map/all_gather | solution.py:67
  27.3 26.9 %while.96 = (s32[]{:T(128)}, f32[16,128]{1,0:T(8,128)S(1)}, f32[16,128]{1,0:T(8,128)S(1)}, f32[2048]{0:T(1024)S(1)}, f32[16,128]{1,0:T(8,128)S(1)}, /*index=5*/f...) while((s32[]{:T(128)}, f32[16,128]{1,0:T(8,128)S(1)}, ...), condition=%wide.region_5.6_spmd, body=%wide.region_2.5_spmd.sunk | while | flops 102760192 | bytes 2397301 | solution.py:37
  54.2 9.1 %pmax.56 = f32[2048]{0:T(1024)S(1)} all-reduce(f32[2048]{0:T(1024)S(1)} %bitcast.240), channel_id=1, replica_groups=mesh['rows'=8,'cols'=4] {'cols'}, use_global_device_ids=true, to_apply=%region_6.7 | all-reduce | flops 2048 | bytes 16384 | tf_op jit(solution)/shard_map/pmax | solution.py:54
  63.3 8.7 %psum.56 = f32[2048]{0:T(1024)S(1)} all-reduce(f32[2048]{0:T(1024)S(1)} %bitcast_multiply_fusion.7), channel_id=1, replica_groups=mesh['rows'=8,'cols'=4] {'cols'}, use_global_device_ids=true, to_apply=%region_7.8 | all-reduce | flops 2048 | bytes 16384 | tf_op jit(solution)/shard_map/psum | solution.py:55
  72.3 26.9 %while.97 = (s32[]{:T(128)}, f32[16,128]{1,0:T(8,128)S(1)}, f32[16,128]{1,0:T(8,128)S(1)}, f32[2048]{0:T(1024)S(1)}, f32[2048]{0:T(1024)S(1)}, /*index=5*/f32[16...) while((s32[]{:T(128)}, f32[16,128]{1,0:T(8,128)S(1)}, ...), condition=%wide.region_11.12_spmd, body=%wide.region_8.11_spmd.sunk | while | flops 102760192 | bytes 2397301 | solution.py:49
  99.2 13.8 %pmax.57 = f32[2048]{0:T(1024)S(1)} all-reduce(f32[2048]{0:T(1024)S(1)} %bitcast.241), channel_id=1, replica_groups=mesh['rows'=8,'cols'=4] {'rows'}, use_global_device_ids=true, to_apply=%region_12.13 | all-reduce | flops 2048 | bytes 16384 | tf_op jit(solution)/shard_map/pmax | solution.py:60
  113.1 13.9 %psum.57 = f32[2048]{0:T(1024)S(1)} all-reduce(f32[2048]{0:T(1024)S(1)} %bitcast_multiply_fusion.6), channel_id=1, replica_groups=mesh['rows'=8,'cols'=4] {'rows'}, use_global_device_ids=true, to_apply=%region_13.14 | all-reduce | flops 2048 | bytes 16384 | tf_op jit(solution)/shard_map/psum | solution.py:61
  127.1 26.9 %while.98 = (s32[]{:T(128)}, f32[16,128]{1,0:T(8,128)S(1)}, f32[16,128]{1,0:T(8,128)S(1)}, f32[2048]{0:T(1024)S(1)}, f32[16,128]{1,0:T(8,128)S(1)}, /*index=5*/f...) while((s32[]{:T(128)}, f32[16,128]{1,0:T(8,128)S(1)}, ...), condition=%wide.region_17.18_spmd, body=%wide.region_14.17_spmd.sunk | while | flops 102760192 | bytes 2397301 | solution.py:37
  127.1 1.3 fusion.90
  130.5 1.3 fusion.90
  133.8 1.3 fusion.90
  137.2 1.3 fusion.90
  140.6 1.3 fusion.90
  143.9 1.3 fusion.90
  147.3 1.3 fusion.90
  150.7 1.3 fusion.90
  154.0 9.1 %pmax.58 = f32[2048]{0:T(1024)S(1)} all-reduce(f32[2048]{0:T(1024)S(1)} %bitcast.242), channel_id=1, replica_groups=mesh['rows'=8,'cols'=4] {'cols'}, use_global_device_ids=true, to_apply=%region_18.19 | all-reduce | flops 2048 | bytes 16384 | tf_op jit(solution)/shard_map/pmax | solution.py:54
  163.1 8.3 %psum.58 = f32[2048]{0:T(1024)S(1)} all-reduce(f32[2048]{0:T(1024)S(1)} %bitcast_multiply_fusion.5), channel_id=1, replica_groups=mesh['rows'=8,'cols'=4] {'cols'}, use_global_device_ids=true, to_apply=%region_19.20 | all-reduce | flops 2048 | bytes 16384 | tf_op jit(solution)/shard_map/psum | solution.py:55
  171.5 26.9 %while.99 = (s32[]{:T(128)}, f32[16,128]{1,0:T(8,128)S(1)}, f32[16,128]{1,0:T(8,128)S(1)}, f32[2048]{0:T(1024)S(1)}, f32[2048]{0:T(1024)S(1)}, /*index=5*/f32[16...) while((s32[]{:T(128)}, f32[16,128]{1,0:T(8,128)S(1)}, ...), condition=%wide.region_23.24_spmd, body=%wide.region_20.23_spmd.sunk | while | flops 102760192 | bytes 2397301 | solution.py:49
  198.4 13.9 %pmax.59 = f32[2048]{0:T(1024)S(1)} all-reduce(f32[2048]{0:T(1024)S(1)} %bitcast.243), channel_id=1, replica_groups=mesh['rows'=8,'cols'=4] {'rows'}, use_global_device_ids=true, to_apply=%region_24.25 | all-reduce | flops 2048 | bytes 16384 | tf_op jit(solution)/shard_map/pmax | solution.py:60
  212.3 13.9 %psum.59 = f32[2048]{0:T(1024)S(1)} all-reduce(f32[2048]{0:T(1024)S(1)} %bitcast_multiply_fusion.4), channel_id=1, replica_groups=mesh['rows'=8,'cols'=4] {'rows'}, use_global_device_ids=true, to_apply=%region_25.26 | all-reduce | flops 2048 | bytes 16384 | tf_op jit(solution)/shard_map/psum | solution.py:61
  226.3 26.9 %while.100 = (s32[]{:T(128)}, f32[16,128]{1,0:T(8,128)S(1)}, f32[16,128]{1,0:T(8,128)S(1)}, f32[2048]{0:T(1024)S(1)}, f32[16,128]{1,0:T(8,128)S(1)}, /*index=5*/...) while((s32[]{:T(128)}, f32[16,128]{1,0:T(8,128)S(1)}, ...), condition=%wide.region_29.30_spmd, body=%wide.region_26.29_spmd.sunk | while | flops 102760192 | bytes 2397301 | solution.py:37
  226.3 1.3 fusion.94
  229.7 1.3 fusion.94
  233.1 1.3 fusion.94
  236.5 1.3 fusion.94
  239.8 1.3 fusion.94
  243.2 1.3 fusion.94
  246.6 1.3 fusion.94
  249.9 1.3 fusion.94
  253.3 9.1 %pmax.60 = f32[2048]{0:T(1024)S(1)} all-reduce(f32[2048]{0:T(1024)S(1)} %bitcast.244), channel_id=1, replica_groups=mesh['rows'=8,'cols'=4] {'cols'}, use_global_device_ids=true, to_apply=%region_30.31 | all-reduce | flops 2048 | bytes 16384 | tf_op jit(solution)/shard_map/pmax | solution.py:54
  262.4 8.7 %psum.60 = f32[2048]{0:T(1024)S(1)} all-reduce(f32[2048]{0:T(1024)S(1)} %bitcast_multiply_fusion.3), channel_id=1, replica_groups=mesh['rows'=8,'cols'=4] {'cols'}, use_global_device_ids=true, to_apply=%region_31.32 | all-reduce | flops 2048 | bytes 16384 | tf_op jit(solution)/shard_map/psum | solution.py:55
  271.2 26.9 %while.101 = (s32[]{:T(128)}, f32[16,128]{1,0:T(8,128)S(1)}, f32[16,128]{1,0:T(8,128)S(1)}, f32[2048]{0:T(1024)S(1)}, f32[2048]{0:T(1024)S(1)}, /*index=5*/f32[1...) while((s32[]{:T(128)}, f32[16,128]{1,0:T(8,128)S(1)}, ...), condition=%wide.region_35.36_spmd, body=%wide.region_32.35_spmd.sunk | while | flops 102760192 | bytes 2397301 | solution.py:49
  298.1 13.9 %pmax.61 = f32[2048]{0:T(1024)S(1)} all-reduce(f32[2048]{0:T(1024)S(1)} %bitcast.245), channel_id=1, replica_groups=mesh['rows'=8,'cols'=4] {'rows'}, use_global_device_ids=true, to_apply=%region_36.37 | all-reduce | flops 2048 | bytes 16384 | tf_op jit(solution)/shard_map/pmax | solution.py:60
  312.1 13.9 %psum.61 = f32[2048]{0:T(1024)S(1)} all-reduce(f32[2048]{0:T(1024)S(1)} %bitcast_multiply_fusion.2), channel_id=1, replica_groups=mesh['rows'=8,'cols'=4] {'rows'}, use_global_device_ids=true, to_apply=%region_37.38 | all-reduce | flops 2048 | bytes 16384 | tf_op jit(solution)/shard_map/psum | solution.py:61
  326.1 26.9 %while.102 = (s32[]{:T(128)}, f32[16,128]{1,0:T(8,128)S(1)}, f32[16,128]{1,0:T(8,128)S(1)}, f32[2048]{0:T(1024)S(1)}, f32[16,128]{1,0:T(8,128)S(1)}, /*index=5*/...) while((s32[]{:T(128)}, f32[16,128]{1,0:T(8,128)S(1)}, ...), condition=%wide.region_41.42_spmd, body=%wide.region_38.41_spmd.sunk | while | flops 102760192 | bytes 2397301 | solution.py:37
  327.8 1.3 fusion.98
  332.8 1.3 fusion.98
  336.2 1.3 fusion.98
  341.2 1.3 fusion.98
  344.6 1.3 fusion.98
  349.7 1.3 fusion.98
  353.0 9.1 %pmax.62 = f32[2048]{0:T(1024)S(1)} all-reduce(f32[2048]{0:T(1024)S(1)} %bitcast.246), channel_id=1, replica_groups=mesh['rows'=8,'cols'=4] {'cols'}, use_global_device_ids=true, to_apply=%region_42.43 | all-reduce | flops 2048 | bytes 16384 | tf_op jit(solution)/shard_map/pmax | solution.py:54
  362.1 8.3 %psum.62 = f32[2048]{0:T(1024)S(1)} all-reduce(f32[2048]{0:T(1024)S(1)} %bitcast_multiply_fusion.1), channel_id=1, replica_groups=mesh['rows'=8,'cols'=4] {'cols'}, use_global_device_ids=true, to_apply=%region_43.44 | all-reduce | flops 2048 | bytes 16384 | tf_op jit(solution)/shard_map/psum | solution.py:55
  370.4 26.9 %while.103 = (s32[]{:T(128)}, f32[16,128]{1,0:T(8,128)S(1)}, f32[16,128]{1,0:T(8,128)S(1)}, f32[2048]{0:T(1024)S(1)}, f32[2048]{0:T(1024)S(1)}, /*index=5*/f32[1...) while((s32[]{:T(128)}, f32[16,128]{1,0:T(8,128)S(1)}, ...), condition=%wide.region_47.48_spmd, body=%wide.region_44.47_spmd.sunk | while | flops 102760192 | bytes 2397301 | solution.py:49
  397.4 13.9 %pmax.63 = f32[2048]{0:T(1024)S(1)} all-reduce(f32[2048]{0:T(1024)S(1)} %bitcast.239), channel_id=1, replica_groups=mesh['rows'=8,'cols'=4] {'rows'}, use_global_device_ids=true, to_apply=%region_48.49 | all-reduce | flops 2048 | bytes 16384 | tf_op jit(solution)/shard_map/pmax | solution.py:60
  411.4 13.9 %psum.63 = f32[2048]{0:T(1024)S(1)} all-reduce(f32[2048]{0:T(1024)S(1)} %bitcast_multiply_fusion), channel_id=1, replica_groups=mesh['rows'=8,'cols'=4] {'rows'}, use_global_device_ids=true, to_apply=%region_49.50 | all-reduce | flops 2048 | bytes 16384 | tf_op jit(solution)/shard_map/psum | solution.py:61
  (661 shorter events, 186.8 us)
Async XLA Ops:
  11.4 0.8 copy-start
  26.6 0.7 copy-start.2
  397.4 13.9 %copy-start.1 = (f32[2048]{0:T(1024)}, f32[2048]{0:T(1024)S(1)}, u32[]{:S(2)}) copy-start(f32[2048]{0:T(1024)S(1)} %get-tuple-element.1228) | copy-start | bytes 24580
where the time goes:
time: 427 us; the launch traced here: 426 us
  blocking collectives  207 us (48%)
  matrix products  163 us (38%)
  other arithmetic  40 us (9%)
  local copies, waits for them, and re-layouts  11.9 us (3%)
    dot_general x128, matrix products, cost_block(): lax.dot_general(left, right, (((0,), (0,)), ((), ())), precision=lax.Prec...  163 us
    psum x4, blocking collectives, finish_cols(): whole_total = lax.psum(total * jnp.exp(peak - whole_peak), 'rows')  55.7 us
    pmax x4, blocking collectives, finish_cols(): whole_peak = lax.pmax(peak, 'rows')  55.6 us
    pmax x4, blocking collectives, finish_rows(): whole_peak = lax.pmax(peak, 'cols')  36.4 us
    psum x4, blocking collectives, finish_rows(): whole_total = lax.psum(total * jnp.exp(peak - whole_peak), 'cols')  34.1 us
    reduce_sum x64, other arithmetic, row_one_block(): return (peak, jnp.sum(jnp.exp(scores - peak[:, None]), axis=1))  19.6 us
    reduce_sum x64, other arithmetic, col_one_block(): return (peak, jnp.sum(jnp.exp(scores - peak[None, :]), axis=0))  19.6 us
    all_gather x1, blocking collectives, body(): targets = lax.all_gather(target_points, 'rows', axis=1, tiled=True)  14.4 us

commit v1 on v0

v1 whole, which is shorter than its diff:
```python
import functools
import math

import jax
import jax.numpy as jnp
from jax import lax
from jax.experimental import pallas as pl
from jax.experimental.pallas import tpu as pltpu
from jax.sharding import PartitionSpec as P

ITERS = 4
EPS = 0.2
ALPHA = math.log2(math.e) / EPS
LANES = 128
SUB = 8
MIB = 1024 * 1024
TILE = 256
LIFT = 50.0

VMEM = pl.BlockSpec(memory_space=pltpu.VMEM)
HBM = pl.BlockSpec(memory_space=pltpu.HBM)
SMEM = pl.BlockSpec(memory_space=pltpu.SMEM)


def tree(op, items):
    items = list(items)
    while len(items) > 1:
        items = [op(*items[k : k + 2]) if k + 1 < len(items) else items[k] for k in range(0, len(items), 2)]
    return items[0]


def lse2(parts):
    peak = tree(jnp.maximum, parts)
    return peak + jnp.log2(tree(jnp.add, [jnp.exp2(part - peak) for part in parts]))


def split3(value):
    high = value.astype(jnp.bfloat16)
    rest = value - high.astype(jnp.float32)
    mid = rest.astype(jnp.bfloat16)
    low = (rest - mid.astype(jnp.float32)).astype(jnp.bfloat16)
    return high, mid, low


def store_rows(ref, row):
    for k in range(row.shape[1] // LANES):
        ref[k : k + 1, :] = row[:, k * LANES : (k + 1) * LANES]


def set_addend(right, first, cols, row):
    high, mid, low = (part.astype(jnp.float32) for part in split3(row))
    index = lax.broadcasted_iota(jnp.int32, (2 * SUB, row.shape[1]), 0)
    rows = jnp.where(index < 3, 1.0, 0.0)
    for k, part in enumerate((high, mid, low)):
        rows = jnp.where(index == 3 + k, part, rows)
    right[first : first + 2 * SUB, cols] = rows.astype(jnp.bfloat16)


def score_tile(left, right, c, t):
    return jnp.dot(
        left[c * TILE : (c + 1) * TILE, :],
        right[:, t * TILE : (t + 1) * TILE],
        preferred_element_type=jnp.float32,
    )


def fold_rows(op, tile):
    return tree(op, [tile[r * SUB : (r + 1) * SUB, :] for r in range(tile.shape[0] // SUB)])


def sweep(left, right, op, change, start, acc):
    width = min(TILE, right.shape[1])

    def step(n, _):
        c = n // (right.shape[1] // width)
        t = n % (right.shape[1] // width)
        cols = pl.ds(pl.multiple_of(t * width, width), width)
        rows = pl.ds(pl.multiple_of(c * TILE, TILE), TILE)
        tile = jnp.dot(left[rows, :], right[:, cols], preferred_element_type=jnp.float32)
        acc[:, cols] = op(acc[:, cols], fold_rows(op, change(tile)))
        return 0

    acc[...] = jnp.full(acc.shape, start, jnp.float32)
    lax.fori_loop(0, left.shape[0] // TILE * (right.shape[1] // width), step, 0)


def exact_lse(left, right, first, acc):
    every = slice(0, right.shape[1])
    set_addend(right, first, every, jnp.zeros((1, right.shape[1]), jnp.float32))
    sweep(left, right, jnp.maximum, lambda tile: tile, -jnp.inf, acc)
    peak = jnp.max(acc[...], axis=0, keepdims=True)
    set_addend(right, first, every, -peak)
    sweep(left, right, jnp.add, jnp.exp2, 0.0, acc)
    return peak + jnp.log2(jnp.sum(acc[...], axis=0, keepdims=True))


def place_sources(x, right, cols):
    depth, width = x.shape
    first = 6 * depth
    high, mid, low = split3(x * (2.0 * ALPHA))
    for k, part in enumerate((high, high, high, mid, mid, low)):
        right[k * depth : (k + 1) * depth, cols] = part
    right[first:, cols] = jnp.zeros((right.shape[0] - first, width), jnp.bfloat16)
    set_addend(right, first, cols, jnp.zeros((1, width), jnp.float32))


def put_rows(ref, start, row):
    for k in range(row.shape[1] // LANES):
        ref[pl.ds(start + k, 1), :] = row[:, k * LANES : (k + 1) * LANES]


def guarded_sums(left, right, first, pieces, lse):
    held = []
    for start, count, row in pieces:
        width = min(TILE, count)
        for t in range(count // width):
            cols = pl.ds(pl.multiple_of(start + t * width, LANES), width)
            held.append((cols, row + t * (width // LANES)))

    def tile(c, cols):
        return jnp.dot(left[c * TILE : (c + 1) * TILE, :], right[:, cols], preferred_element_type=jnp.float32)

    peaks = []
    for cols, _ in held:
        peak = jnp.max(fold_rows(jnp.maximum, tile(0, cols)), axis=0, keepdims=True)
        peaks.append(peak)
    for (cols, _), peak in zip(held, peaks):
        set_addend(right, first, cols, -peak)
    totals = []
    for cols, _ in held:
        total = None
        for c in range(left.shape[0] // TILE):
            part = fold_rows(jnp.add, jnp.exp2(tile(c, cols)))
            total = part if total is None else total + part
        totals.append(jnp.sum(total, axis=0, keepdims=True))
    for (_, row), peak, total in zip(held, peaks, totals):
        put_rows(lse, row, peak + jnp.log2(total))
    return jnp.max(tree(jnp.maximum, totals)) < 2.0**100


def place_pieces(points, index, pieces):
    width = pieces[0].shape[1]
    for distance, piece in enumerate(pieces):
        start = pl.multiple_of((index ^ distance) * width, LANES)
        points[:, pl.ds(start, width)] = piece[...]


def own_scores_kernel(place, own_tgt, own_g0, src, *refs):
    lse, norms, left, right, stack, points, acc, held_tgt, g0, sems = refs[-10:]
    tgt = refs[:-10]
    copies = [
        pltpu.make_async_copy(source, target, sems.at[k])
        for k, (source, target) in enumerate(((own_tgt, held_tgt), (own_g0, g0)))
    ]
    for copy in copies:
        copy.start()
    depth, width = src.shape
    first = 6 * depth
    x = src[...]
    store_rows(norms, jnp.sum(x * x, axis=0, keepdims=True))
    place_sources(x, right, slice(0, width))
    for copy in copies:
        copy.wait()

    place_pieces(points, place[1], (held_tgt, *tgt))
    ntgt = left.shape[0]
    y = points[...]
    gamma = ALPHA * (g0[...] - jnp.sum(y * y, axis=0, keepdims=True))
    high, mid, low = split3(y)
    for k, part in enumerate((high, mid, low, high, mid, high)):
        stack[k * depth : (k + 1) * depth, :] = part
    index = lax.broadcasted_iota(jnp.int32, (stack.shape[0] - first, ntgt), 0)
    rows = jnp.where((index >= 3) & (index < 6), 1.0, 0.0)
    for k, part in enumerate(split3(gamma)):
        rows = jnp.where(index == k, part.astype(jnp.float32), rows)
    stack[first:, :] = rows.astype(jnp.bfloat16)
    for c in range(ntgt // TILE):
        left[c * TILE : (c + 1) * TILE, :] = stack[:, c * TILE : (c + 1) * TILE].T

    fine = guarded_sums(left, right, first, [(0, width, 0)], lse)

    @pl.when(jnp.logical_not(fine))
    def _():
        store_rows(lse, exact_lse(left, right, first, acc))


def scores_kernel(place, left, own_right, own_lse, own_norms, *refs):
    lse, norms, right, acc = refs[-4:]
    src = refs[:-4]
    depth, width = src[0].shape
    first = 6 * depth
    own = place[0] * width
    right[:, pl.ds(pl.multiple_of(own, LANES), width)] = own_right[...]
    pieces = []
    for distance, piece in enumerate(src, 1):
        owner = place[0] ^ distance
        start = owner * width
        row = owner * (width // LANES)
        x = piece[...]
        put_rows(norms, row, jnp.sum(x * x, axis=0, keepdims=True))
        place_sources(x, right, pl.ds(pl.multiple_of(start, LANES), width))
        pieces.append((start, width, row))
    fine = guarded_sums(left, right, first, pieces, lse)

    @pl.when(jnp.logical_not(fine))
    def _():
        store_rows(lse, exact_lse(left, right, first, acc))

    for k in range(width // LANES):
        row = pl.ds(place[0] * (width // LANES) + k, 1)
        lse[row, :] = own_lse[k : k + 1, :]
        norms[row, :] = own_norms[k : k + 1, :]


def read_row(ref, k):
    return ref[k : k + 1, :]


QUARTER = LANES // 4


def lane_mask(index):
    return lax.broadcasted_iota(jnp.int32, (SUB, LANES), 1) == index


def group(index):
    return pl.ds(pl.multiple_of(index * SUB, SUB), SUB)


def join_chains(chains):
    lanes = lax.broadcasted_iota(jnp.int32, (SUB, LANES), 1)
    value = chains[-1]
    for k in reversed(range(len(chains) - 1)):
        value = jnp.where(lanes < (k + 1) * QUARTER, chains[k], value)
    return value


def fold_lanes(reduce, partial, out, wide=None):
    for h in range(out.shape[0] // SUB):
        chains = []
        for index in range(LANES):
            rows = slice((h * LANES + index) * SUB, (h * LANES + index + 1) * SUB)
            value = reduce(partial[rows, :], axis=1, keepdims=True)
            if wide is not None:
                wide[rows, :] = jnp.broadcast_to(value, (SUB, LANES))
            if index % QUARTER == 0:
                chains.append(jnp.broadcast_to(value, (SUB, LANES)))
            else:
                chains[-1] = jnp.where(lane_mask(index), value, chains[-1])
        out[h * SUB : (h + 1) * SUB, :] = join_chains(chains)


def first_columns_kernel(log_ntgt, first, left, _, row_lse, ratios, right, phi, peaks, lse, partial, wide, sums):
    phi[...] = log_ntgt - row_lse[...]
    for k in range(phi.shape[0]):
        set_addend(right, first, slice(k * LANES, (k + 1) * LANES), read_row(phi, k) + LIFT)
    halves = TILE // LANES
    for t in range(ratios.shape[1] // TILE):
        for c in range(ratios.shape[0] // TILE):
            rows = slice(c * TILE, (c + 1) * TILE)
            tile = jnp.exp2(score_tile(left, right, c, t))
            ratios[rows, t * TILE : (t + 1) * TILE] = tile
            part = tree(jnp.add, [tile[:, k * LANES : (k + 1) * LANES] for k in range(halves)])
            partial[rows, :] = part if t == 0 else partial[rows, :] + part
    fold_lanes(jnp.sum, partial, sums)
    peaks[...] = jnp.zeros(peaks.shape, jnp.float32)

    @pl.when(jnp.logical_not(jnp.min(sums[...]) >= 2.0**-20))
    def _():
        groups = ratios.shape[0] // SUB
        few = 4

        def score_step(n, _):
            c = n // (ratios.shape[1] // TILE)
            t = n % (ratios.shape[1] // TILE)
            cols = pl.ds(pl.multiple_of(t * TILE, TILE), TILE)
            rows = pl.ds(pl.multiple_of(c * TILE, TILE), TILE)
            ratios[rows, cols] = jnp.dot(left[rows, :], right[:, cols], preferred_element_type=jnp.float32)
            return 0

        def peak_step(c, _):
            for t in range(few):
                rows = group(c * few + t)
                partial[rows, :] = tree(
                    jnp.maximum, [ratios[rows, k * LANES : (k + 1) * LANES] for k in range(ratios.shape[1] // LANES)]
                )
            return 0

        def ratio_step(c, _):
            for t in range(few):
                rows = group(c * few + t)
                peak = wide[rows, :]
                tiles = [
                    jnp.exp2(ratios[rows, k * LANES : (k + 1) * LANES] - peak)
                    for k in range(ratios.shape[1] // LANES)
                ]
                for k, value in enumerate(tiles):
                    ratios[rows, k * LANES : (k + 1) * LANES] = value
                partial[rows, :] = tree(jnp.add, tiles)
            return 0

        lax.fori_loop(0, ratios.shape[0] // TILE * (ratios.shape[1] // TILE), score_step, 0)
        lax.fori_loop(0, groups // few, peak_step, 0)
        fold_lanes(jnp.max, partial, peaks, wide)
        lax.fori_loop(0, groups // few, ratio_step, 0)
        fold_lanes(jnp.sum, partial, sums)

    lse[...] = peaks[...] + (jnp.log2(sums[...]) - LIFT)


def row_sums(ratios, weights, out):
    count = ratios.shape[1]
    total = jnp.zeros((SUB, count), jnp.float32)
    for h in range(weights.shape[0] // SUB):
        held = weights[h * SUB : (h + 1) * SUB, :]
        for index in range(LANES):
            rows = slice((h * LANES + index) * SUB, (h * LANES + index + 1) * SUB)
            total = total + ratios[rows, :] * jnp.broadcast_to(held[:, index : index + 1], (SUB, count))
    store_rows(out, jnp.sum(total, axis=0, keepdims=True))


def first_rows_kernel(log_nsrc, ratios, peaks, col_lse, out, weights, base):
    shift = log_nsrc - col_lse[...]
    base[...] = shift
    weights[...] = jnp.exp2(peaks[...] + (shift - LIFT))
    row_sums(ratios, weights[...], out)


def rows_kernel(nsrc, ratios, weights, total, out):
    row_sums(ratios, weights[...] * (nsrc / total[...]), out)


def columns_kernel(ntgt, ratios, weights, total, out, scale):
    total = total[...]
    scale[...] = ntgt / total
    count = ratios.shape[1]
    tiles = count // LANES
    scales = jnp.concatenate([jnp.broadcast_to(read_row(scale, k), (SUB, LANES)) for k in range(tiles)], axis=1)
    for h in range(out.shape[0] // SUB):
        chains = []
        for index in range(LANES):
            rows = slice((h * LANES + index) * SUB, (h * LANES + index + 1) * SUB)
            value = jnp.sum(ratios[rows, :] * scales, axis=1, keepdims=True)
            if index % QUARTER == 0:
                chains.append(jnp.broadcast_to(value, (SUB, LANES)))
            else:
                chains[-1] = jnp.where(lane_mask(index), value, chains[-1])
        rows = slice(h * SUB, (h + 1) * SUB)
        out[rows, :] = join_chains(chains) * weights[rows, :]


def finish_kernel(log_nsrc, base, total, out):
    out[...] = (base[...] + (log_nsrc - jnp.log2(total[...]))) * (1.0 / ALPHA)


def swap(value, axis, distance):
    return lax.ppermute(value, axis, [(k, k ^ distance) for k in range(lax.axis_size(axis))])


def hop(value, distance, lead, step=1):
    nrows, ncols = lax.axis_size("rows"), lax.axis_size("cols")
    perm = []
    for row in range(nrows):
        for col in range(step - 1, ncols, step):
            other = col ^ distance
            perm.append((row * ncols + col, lead(row, col, other) * ncols + other))
    return lax.ppermute(value, ("rows", "cols"), perm)


def to_block(value, distance, odd=False):
    return hop(value, distance, lambda row, col, other: row ^ (other & 1), 1 + odd)


def same_block(value, distance):
    return hop(value, distance, lambda row, col, other: row ^ ((col ^ other) & 1))


def combine_cols(reduce, value):
    return reduce([value] + [same_block(value, d) for d in range(1, lax.axis_size("cols"))])


def combine_rows(reduce, value):
    value = reduce([value, swap(value, "rows", 1)])
    return reduce([value] + [swap(value, "rows", d) for d in range(3, lax.axis_size("rows"), 2)])


def add_all(values):
    return tree(jnp.add, values)


def gather_rows(value):
    far = {0: value}
    for d in range(3, lax.axis_size("rows"), 2):
        far[d] = swap(value, "rows", d)
    pieces = dict(far)
    for d, piece in far.items():
        pieces[d ^ 1] = swap(piece, "rows", 1)
    return [pieces[d] for d in range(1, lax.axis_size("rows"))]


def call(kernel, out_shape, nin, scratch=(), limit=8, aliases=None, smem=0, hbm=0):
    return pl.pallas_call(
        kernel,
        out_shape=out_shape,
        in_specs=[SMEM] * smem + [HBM] * hbm + [VMEM] * (nin - smem - hbm),
        out_specs=[VMEM] * len(out_shape),
        scratch_shapes=list(scratch),
        input_output_aliases=aliases or {},
        compiler_params=pltpu.CompilerParams(vmem_limit_bytes=limit * MIB),
    )


def body(source_points, target_points, target_init):
    ncols = lax.axis_size("cols")
    nrows = lax.axis_size("rows")
    depth = source_points.shape[0]
    src_count = source_points.shape[1] * ncols
    tgt_count = target_points.shape[1] * nrows
    nsrc = src_count * nrows
    ntgt = tgt_count * ncols
    log_nsrc = math.log2(nsrc)
    log_ntgt = math.log2(ntgt)
    stack = -(-(6 * depth + 2 * SUB) // LANES) * LANES
    f32 = jnp.float32
    by_src = jax.ShapeDtypeStruct((src_count // LANES, LANES), f32)
    by_tgt = jax.ShapeDtypeStruct((tgt_count // LANES, LANES), f32)
    square = pltpu.VMEM((tgt_count, src_count), f32)
    wide = pltpu.VMEM((tgt_count, LANES), f32)
    row_src = pltpu.VMEM(by_src.shape, f32)
    row_tgt = pltpu.VMEM(by_tgt.shape, f32)

    def pin(value):
        return pltpu.with_memory_space_constraint(value, pltpu.VMEM)

    targets = gather_rows(target_points)
    sources = [to_block(source_points, d) for d in range(ncols)]
    place = jnp.stack([lax.axis_index("cols"), lax.axis_index("rows")]).astype(jnp.int32)
    bf16 = jnp.bfloat16
    piece = source_points.shape[1]
    by_piece = jax.ShapeDtypeStruct((piece // LANES, LANES), f32)
    own_lse, own_norms, left, own_right = call(
        own_scores_kernel,
        [by_piece, by_piece, pltpu.VMEM((tgt_count, stack), bf16), pltpu.VMEM((stack, piece), bf16)],
        3 + nrows,
        [
            pltpu.VMEM((stack, tgt_count), bf16),
            pltpu.VMEM((depth, tgt_count), f32),
            pltpu.VMEM((SUB, piece), f32),
            pltpu.VMEM(target_points.shape, f32),
            pltpu.VMEM((1, tgt_count), f32),
            pltpu.SemaphoreType.DMA((2,)),
        ],
        limit=16,
        smem=1,
        hbm=2,
    )(
        place,
        *(
            pltpu.with_memory_space_constraint(own, pltpu.HBM)
            for own in (target_points, target_init.reshape(1, tgt_count))
        ),
        sources[0],
        *targets,
    )
    left = pin(left)
    lse, norms, right = call(
        scores_kernel,
        [by_src, by_src, pltpu.VMEM((stack, src_count), bf16)],
        4 + ncols,
        [pltpu.VMEM((SUB, src_count), f32)],
        limit=16,
        smem=1,
    )(place, left, pin(own_right), own_lse, own_norms, *sources[1:])
    ratios, _, phi, peaks, lse = call(
        functools.partial(first_columns_kernel, log_ntgt, 6 * depth),
        [square, pltpu.VMEM((stack, src_count), jnp.bfloat16), by_src, by_tgt, by_tgt],
        3,
        [wide, wide, row_tgt],
        aliases={1: 1},
    )(left, pin(right), combine_cols(lse2, lse))
    ratios = pin(ratios)
    total, weights, base = call(
        functools.partial(first_rows_kernel, log_nsrc),
        [by_src, by_tgt, by_tgt],
        3,
    )(ratios, peaks, combine_rows(lse2, lse))
    for step in range(1, ITERS):
        row_total = combine_cols(add_all, total)
        (total,) = call(
            functools.partial(columns_kernel, float(ntgt)),
            [by_tgt],
            3,
            [row_src],
        )(ratios, weights, row_total)
        if step == ITERS - 1:
            total, row_total = lax.optimization_barrier((total, row_total))
        total = combine_rows(add_all, total)
        if step < ITERS - 1:
            (total,) = call(
                functools.partial(rows_kernel, float(nsrc)),
                [by_src],
                3,
            )(ratios, weights, total)
    f = (phi + (log_ntgt - jnp.log2(row_total))) * (1.0 / ALPHA) + norms
    f = jnp.where(lax.axis_index("cols") % 2 == 1, to_block(f, 0, odd=True), f)
    (delta,) = call(functools.partial(finish_kernel, log_nsrc), [by_tgt], 2)(base, total)
    delta = delta.reshape(-1, SUB, LANES).transpose(0, 2, 1).reshape(-1)
    return f.reshape(-1), target_init + delta


def solution(mesh):
    in_specs = (P(None, ("rows", "cols")), P(None, ("cols", "rows")), P("cols"))
    out_specs = (P("rows"), P("cols"))
    return jax.shard_map(body, mesh=mesh, in_specs=in_specs, out_specs=out_specs, check_vma=False)
```

time: 427 us -> 135 us (0.32)
  blocking collectives: 207 us -> 0 us
  matrix products: 163 us -> 0 us
  Pallas kernels: 0 us -> 67.7 us
  starting transfers between devices: 0 us -> 40.8 us
  other arithmetic: 40 us -> 1.4 us
  waiting for transfers between devices: 0 us -> 23.9 us
  local copies, waits for them, and re-layouts: 11.9 us -> 0.24 us
    dot_general x128 -> x0, matrix products: 163 us -> none  [cost_block(): lax.dot_general(left, right, (((0,), (0,)), ((), ())), precision=lax.Prec...]
    pmax x8 -> x0, blocking collectives: 92 us -> none  [the longest x4 55.6 us: finish_cols(): whole_peak = lax.pmax(peak, 'rows')]
    psum x8 -> x0, blocking collectives: 89.8 us -> none  [the longest x4 55.7 us: finish_cols(): whole_total = lax.psum(total * jnp.exp(peak - whole_peak), 'rows')]
    pallas_call x0 -> x10, Pallas kernels: none -> 67.7 us  [the longest x1 29.2 us: body(): call(scores_kernel, [by_src, by_src, pltpu.VMEM((stack, src_count), bf16)...]
    ppermute x0 -> x40, starting transfers between devices: none -> 40.8 us  [the longest x23 22.5 us: swap(): lax.ppermute(value, axis, [(k, k ^ distance) for k in range(lax.axis_size...]
    reduce_sum x130 -> x0, other arithmetic: 39.3 us -> none  [the longest x64 19.6 us: row_one_block(): return (peak, jnp.sum(jnp.exp(scores - peak[:, None]), axis=1))]
    all_gather x2 -> x0, blocking collectives: 25.1 us -> none  [the longest x1 14.4 us: body(): targets = lax.all_gather(target_points, 'rows', axis=1, tiled=True)]
    ppermute x0 -> x40, waiting for transfers between devices: none -> 23.9 us  [the longest x23 14 us: swap(): lax.ppermute(value, axis, [(k, k ^ distance) for k in range(lax.axis_size...]
  transfers between devices with their start and end apart: 0 -> 40, of which waited for: 0 -> 26; matrix products, arithmetic and copies ran while one was open for 0% -> 1% of each run, Pallas kernels for 0% -> 7%
where the time goes in v1:
time: 135 us
  Pallas kernels  67.7 us (50%)
  starting transfers between devices  40.8 us (30%)
  waiting for transfers between devices  23.9 us (18%)
  other arithmetic  1.4 us (1%)
    pallas_call x1, Pallas kernels, body(): call(scores_kernel, [by_src, by_src, pltpu.VMEM((stack, src_count), bf16)...  29.2 us
    ppermute x23, starting transfers between devices, swap(): lax.ppermute(value, axis, [(k, k ^ distance) for k in range(lax.axis_size...  22.5 us
    pallas_call x1, Pallas kernels, body(): call(functools.partial(first_columns_kernel, log_ntgt, 6 * depth), [squar...  22.3 us
    ppermute x17, starting transfers between devices, hop(): return lax.ppermute(value, ('rows', 'cols'), perm)  18.3 us
    ppermute x23, waiting for transfers between devices, swap(): lax.ppermute(value, axis, [(k, k ^ distance) for k in range(lax.axis_size...  14 us
    ppermute x17, waiting for transfers between devices, hop(): return lax.ppermute(value, ('rows', 'cols'), perm)  9.86 us
    pallas_call x1, Pallas kernels, body(): call(own_scores_kernel, [by_piece, by_piece, pltpu.VMEM((tgt_count, stack...  8.94 us
    pallas_call x3, Pallas kernels, body(): call(functools.partial(columns_kernel, float(ntgt)), [by_tgt], 3, [row_src])  3.64 us
  transfers between devices with their start and end apart: 40, of which 26 were waited for; matrix products, arithmetic and copies ran while one was open for 1% of the time, Pallas kernels for 7%

profile of v1, /device:TPU:0, one launch (start us, length us, event | category | flops | bytes accessed | tf_op | source)
XLA Modules:
  0.0 134.8 jit_solution(211357358333121841)
XLA Ops:
  0.6 3.5 %collective-permute-start.4 = (f32[32,256]{1,0:T(8,128)}, f32[32,256]{1,0:T(8,128)S(1)}, u32[]{:S(2)}, u32[]{:S(2)}) collective-permute-start(f32[32,256]{1,0:T(8,128)} %own_tgt.1), channel_id=1, source_target_pairs={{0,20},{4,16},{8,28},{12,24},{16,4},{20,0},{24,12},{28,8},{1,21},{... | collective-permute-start | bytes 98312 | tf_op jit(solution)/shard_map/ppermute | solution.py:357
  4.2 1.9 %collective-permute-start.2 = (f32[32,256]{1,0:T(8,128)}, f32[32,256]{1,0:T(8,128)S(1)}, u32[]{:S(2)}, u32[]{:S(2)}) collective-permute-start(f32[32,256]{1,0:T(8,128)} %own_tgt.1), channel_id=1, source_target_pairs={{0,12},{4,8},{8,4},{12,0},{16,28},{20,24},{24,20},{28,16},{1,13},{... | collective-permute-start | bytes 98312 | tf_op jit(solution)/shard_map/ppermute | solution.py:357
  6.7 1.3 collective-permute-done.2.refs_2_
  8.4 1.2 collective-permute-start.8
  9.6 1.5 %collective-permute-start = (f32[32,512]{1,0:T(8,128)}, f32[32,512]{1,0:T(8,128)S(1)}, u32[]{:S(2)}, u32[]{:S(2)}) collective-permute-start(f32[32,512]{1,0:T(8,128)} %param.3), channel_id=1, source_target_pairs={{0,0},{1,5},{2,2},{3,7},{4,4},{5,1},{6,6},{7,3},{8,8},{9,13},{10,1... | collective-permute-start | bytes 196616 | tf_op jit(solution)/shard_map/ppermute | solution.py:367
  11.4 2.6 %collective-permute-start.10 = (f32[32,512]{1,0:T(8,128)}, f32[32,512]{1,0:T(8,128)S(1)}, u32[]{:S(2)}, u32[]{:S(2)}) collective-permute-start(f32[32,512]{1,0:T(8,128)} %param.3), channel_id=1, source_target_pairs={{0,7},{1,2},{2,5},{3,0},{4,3},{5,6},{6,1},{7,4},{8,15},{9,10},{10,... | collective-permute-start | bytes 196616 | tf_op jit(solution)/shard_map/ppermute | solution.py:367
  14.5 1.1 collective-permute-done.7.refs_5_
  15.7 8.9 %shard_map.50 = (f32[4,128]{1,0:T(4,128)S(1)}, f32[4,128]{1,0:T(4,128)S(1)}, bf16[2048,256]{1,0:T(8,128)(2,1)S(1)}, bf16[256,512]{1,0:T(8,128)(2,1)S(1)}) custom-call(s32[2]{0:T(128)S(1)} %pad_add_fusion.place, f32[32,256]{1,0:T(8,128)} %own_tgt.1, f32[1,2048]{1,0:T(1,128)} %bitcast.9, f32[32,512]{1,0:T(8,128)S(1)} %collective-permute-done.src, ...), custom_call_target="tpu_custom_call" | custom-call | tf_op jit(solution)/shard_map/pallas_call | solution.py:441
  24.6 29.2 %shard_map.51 = (f32[16,128]{1,0:T(8,128)S(1)}, f32[16,128]{1,0:T(8,128)S(1)}, bf16[256,2048]{1,0:T(8,128)(2,1)S(1)}) custom-call(s32[2]{0:T(128)S(1)} %pad_add_fusion.place, bf16[2048,256]{1,0:T(8,128)(2,1)S(1)} %get-tuple-element.18.left, bf16[256,512]{1,0:T(8,128)(2,1)S(1)} %get-tuple-element.19.own_right, f32[4,128]{1,0:T(4,128)S(1)} %get-tuple-element.20.own_lse, ...), custom_call_target="tpu_custom_call" | custom-call | tf_op jit(solution)/shard_map/pallas_call | solution.py:466
  53.9 1.2 collective-permute-start.13
  55.6 1.3 collective-permute-start.11
  56.9 1.0 collective-permute-done.13
  57.9 0.8 collective-permute-done.12
  58.7 22.3 %shard_map.52 = (f32[2048,2048]{1,0:T(8,128)S(1)}, bf16[256,2048]{1,0:T(8,128)(2,1)S(1)}, f32[16,128]{1,0:T(8,128)S(1)}, f32[16,128]{1,0:T(8,128)S(1)}, f32[16,128]{1,0:T(8,128)S(1)}) custom-call(bf16[2048,256]{1,0:T(8,128)(2,1)S(1)} %get-tuple-element.18.left, bf16[256,2048]{1,0:T(8,128)(2,1)S(1)} %get-tuple-element.22._, ...), custom_call_target="tpu_custom_call", output_to_operand_aliasing={{1}: (1, {})} | custom-call | tf_op jit(solution)/shard_map/pallas_call | solution.py:474
  81.2 1.1 collective-permute-done.14
  82.3 2.9 %collective-permute-start.17 = (f32[16,128]{1,0:T(8,128)S(1)}, f32[16,128]{1,0:T(8,128)S(1)}, u32[]{:S(2)}, u32[]{:S(2)}) collective-permute-start(f32[16,128]{1,0:T(8,128)S(1)} %multiply_add_fusion.2), channel_id=1, source_target_pairs={{0,28},{4,24},{8,20},{12,16},{16,12},{20,8},{24,4},{28,0},{1,29},{... | collective-permute-start | bytes 24584 | tf_op jit(solution)/shard_map/ppermute | solution.py:357
  85.1 1.1 collective-permute-start.15
  86.2 1.0 collective-permute-done.17
  87.2 1.9 %collective-permute-done.16 = f32[16,128]{1,0:T(8,128)S(1)} collective-permute-done((f32[16,128]{1,0:T(8,128)S(1)}, f32[16,128]{1,0:T(8,128)S(1)}, u32[]{:S(2)}, u32[]{:S(2)}) %collective-permute-start.16) | collective-permute-done | bytes 8224 | tf_op jit(solution)/shard_map/ppermute | solution.py:357
  89.1 1.2 shard_map.53
  90.3 2.3 %collective-permute-start.20 = (f32[16,128]{1,0:T(8,128)S(1)}, f32[16,128]{1,0:T(8,128)S(1)}, u32[]{:S(2)}, u32[]{:S(2)}) collective-permute-start(f32[16,128]{1,0:T(8,128)S(1)} %get-tuple-element.29), channel_id=1, source_target_pairs={{0,7},{1,6},{2,5},{3,4},{4,3},{5,2},{6,1},{7,0},{8,15},{9,14},{10,... | collective-permute-start | bytes 24584 | tf_op jit(solution)/shard_map/ppermute | solution.py:367
  93.3 1.0 collective-permute-done.20
  94.4 1.9 %collective-permute-done.19 = f32[16,128]{1,0:T(8,128)S(1)} collective-permute-done((f32[16,128]{1,0:T(8,128)S(1)}, f32[16,128]{1,0:T(8,128)S(1)}, u32[]{:S(2)}, u32[]{:S(2)}) %collective-permute-start.19) | collective-permute-done | bytes 8224 | tf_op jit(solution)/shard_map/ppermute | solution.py:367
  96.3 1.2 shard_map.54
  97.7 1.1 collective-permute-done.21
  98.7 1.2 collective-permute-start.24
  100.5 2.2 %collective-permute-start.22 = (f32[16,128]{1,0:T(8,128)S(1)}, f32[16,128]{1,0:T(8,128)S(1)}, u32[]{:S(2)}, u32[]{:S(2)}) collective-permute-start(f32[16,128]{1,0:T(8,128)S(1)} %add.120), channel_id=1, source_target_pairs={{0,12},{4,8},{8,4},{12,0},{16,28},{20,24},{24,20},{28,16},{1,13},{... | collective-permute-start | bytes 24584 | tf_op jit(solution)/shard_map/ppermute | solution.py:357
  102.6 1.0 collective-permute-done.24
  104.1 1.2 shard_map.55
  105.3 1.4 %collective-permute-start.27 = (f32[16,128]{1,0:T(8,128)S(1)}, f32[16,128]{1,0:T(8,128)S(1)}, u32[]{:S(2)}, u32[]{:S(2)}) collective-permute-start(f32[16,128]{1,0:T(8,128)S(1)} %shard_map.55), channel_id=1, source_target_pairs={{0,7},{1,6},{2,5},{3,4},{4,3},{5,2},{6,1},{7,0},{8,15},{9,14},{10,... | collective-permute-start | bytes 24584 | tf_op jit(solution)/shard_map/ppermute | solution.py:367
  107.3 1.0 collective-permute-start.25
  108.3 1.0 collective-permute-done.27
  109.4 1.0 collective-permute-done.26
  110.4 1.2 shard_map.56
  111.8 1.1 collective-permute-done.28
  112.9 2.1 %collective-permute-start.31 = (f32[16,128]{1,0:T(8,128)S(1)}, f32[16,128]{1,0:T(8,128)S(1)}, u32[]{:S(2)}, u32[]{:S(2)}) collective-permute-start(f32[16,128]{1,0:T(8,128)S(1)} %add.127), channel_id=1, source_target_pairs={{0,28},{4,24},{8,20},{12,16},{16,12},{20,8},{24,4},{28,0},{1,29},{... | collective-permute-start | bytes 24584 | tf_op jit(solution)/shard_map/ppermute | solution.py:357
  115.0 0.8 collective-permute-start.30
  115.8 1.0 collective-permute-start.29
  116.7 1.0 collective-permute-done.31
  117.7 1.2 collective-permute-done.30
  119.0 1.2 shard_map.57
  120.2 2.3 %collective-permute-start.34 = (f32[16,128]{1,0:T(8,128)S(1)}, f32[16,128]{1,0:T(8,128)S(1)}, u32[]{:S(2)}, u32[]{:S(2)}) collective-permute-start(f32[16,128]{1,0:T(8,128)S(1)} %shard_map.57), channel_id=1, source_target_pairs={{0,7},{1,6},{2,5},{3,4},{4,3},{5,2},{6,1},{7,0},{8,15},{9,14},{10,... | collective-permute-start | bytes 24584 | tf_op jit(solution)/shard_map/ppermute | solution.py:367
  123.2 1.0 collective-permute-done.34
  124.2 1.9 %collective-permute-done.33 = f32[16,128]{1,0:T(8,128)S(1)} collective-permute-done((f32[16,128]{1,0:T(8,128)S(1)}, f32[16,128]{1,0:T(8,128)S(1)}, u32[]{:S(2)}, u32[]{:S(2)}) %collective-permute-start.33) | collective-permute-done | bytes 8224 | tf_op jit(solution)/shard_map/ppermute | solution.py:367
  126.1 1.2 shard_map.58
  128.5 1.3 collective-permute-start.39
  129.9 0.8 collective-permute-start.38
  130.7 1.8 %collective-permute-start.37 = (f32[16,128]{1,0:T(8,128)S(1)}, f32[16,128]{1,0:T(8,128)S(1)}, u32[]{:S(2)}, u32[]{:S(2)}) collective-permute-start(f32[16,128]{1,0:T(8,128)S(1)} %add.136), channel_id=1, source_target_pairs={{0,12},{4,8},{8,4},{12,0},{16,28},{20,24},{24,20},{28,16},{1,13},{... | collective-permute-start | bytes 24584 | tf_op jit(solution)/shard_map/ppermute | solution.py:357
  (62 shorter events, 9.9 us)
Async XLA Ops:
  0.6 5.6 %collective-permute-start.4 = (f32[32,256]{1,0:T(8,128)}, f32[32,256]{1,0:T(8,128)S(1)}, u32[]{:S(2)}, u32[]{:S(2)}) collective-permute-start(f32[32,256]{1,0:T(8,128)} %own_tgt.1), channel_id=1, source_target_pairs={{0,20},{4,16},{8,28},{12,24},{16,4},{20,0},{24,12},{28,8},{1,21},{... | collective-permute-start | bytes 98312 | tf_op jit(solution)/shard_map/ppermute | solution.py:357
  4.2 3.8 %collective-permute-start.2 = (f32[32,256]{1,0:T(8,128)}, f32[32,256]{1,0:T(8,128)S(1)}, u32[]{:S(2)}, u32[]{:S(2)}) collective-permute-start(f32[32,256]{1,0:T(8,128)} %own_tgt.1), channel_id=1, source_target_pairs={{0,12},{4,8},{8,4},{12,0},{16,28},{20,24},{24,20},{28,16},{1,13},{... | collective-permute-start | bytes 98312 | tf_op jit(solution)/shard_map/ppermute | solution.py:357
  6.0 3.5 %collective-permute-start.1 = (f32[32,256]{1,0:T(8,128)}, f32[32,256]{1,0:T(8,128)S(1)}, u32[]{:S(2)}, u32[]{:S(2)}) collective-permute-start(f32[32,256]{1,0:T(8,128)} %own_tgt.1), channel_id=1, source_target_pairs={{0,4},{4,0},{8,12},{12,8},{16,20},{20,16},{24,28},{28,24},{1,5},{5... | collective-permute-start | bytes 98312 | tf_op jit(solution)/shard_map/ppermute | solution.py:357
  6.0 5.3 %collective-permute-start.6 = (f32[32,256]{1,0:T(8,128)}, f32[32,256]{1,0:T(8,128)S(1)}, u32[]{:S(2)}, u32[]{:S(2)}) collective-permute-start(f32[32,256]{1,0:T(8,128)} %own_tgt.1), channel_id=1, source_target_pairs={{0,28},{4,24},{8,20},{12,16},{16,12},{20,8},{24,4},{28,0},{1,29},{... | collective-permute-start | bytes 98312 | tf_op jit(solution)/shard_map/ppermute | solution.py:357
  6.3 7.7 %collective-permute-start.5 = (f32[32,256]{1,0:T(8,128)S(1)}, f32[32,256]{1,0:T(8,128)S(1)}, u32[]{:S(2)}, u32[]{:S(2)}) collective-permute-start(f32[32,256]{1,0:T(8,128)S(1)} %collective-permute-done.4.refs_4_), channel_id=1, source_target_pairs={{0,4},{4,0},{8,12},{12,8},{16,20},{20,16},{24,28},{28,24},{1,5},{5... | collective-permute-start | bytes 98312 | tf_op jit(solution)/shard_map/ppermute | solution.py:357
  8.0 6.5 %collective-permute-start.3 = (f32[32,256]{1,0:T(8,128)S(1)}, f32[32,256]{1,0:T(8,128)S(1)}, u32[]{:S(2)}, u32[]{:S(2)}) collective-permute-start(f32[32,256]{1,0:T(8,128)S(1)} %collective-permute-done.2.refs_2_), channel_id=1, source_target_pairs={{0,4},{4,0},{8,12},{12,8},{16,20},{20,16},{24,28},{28,24},{1,5},{5... | collective-permute-start | bytes 98312 | tf_op jit(solution)/shard_map/ppermute | solution.py:357
  8.4 16.2 %collective-permute-start.8 = (f32[32,512]{1,0:T(8,128)}, f32[32,512]{1,0:T(8,128)S(1)}, u32[]{:S(2)}, u32[]{:S(2)}) collective-permute-start(f32[32,512]{1,0:T(8,128)} %param.3), channel_id=1, source_target_pairs={{0,5},{1,0},{2,7},{3,2},{4,1},{5,4},{6,3},{7,6},{8,13},{9,8},{10,1... | collective-permute-start | bytes 196616 | tf_op jit(solution)/shard_map/ppermute | solution.py:367
  9.6 6.1 %collective-permute-start = (f32[32,512]{1,0:T(8,128)}, f32[32,512]{1,0:T(8,128)S(1)}, u32[]{:S(2)}, u32[]{:S(2)}) collective-permute-start(f32[32,512]{1,0:T(8,128)} %param.3), channel_id=1, source_target_pairs={{0,0},{1,5},{2,2},{3,7},{4,4},{5,1},{6,6},{7,3},{8,8},{9,13},{10,1... | collective-permute-start | bytes 196616 | tf_op jit(solution)/shard_map/ppermute | solution.py:367
  11.4 13.2 %collective-permute-start.10 = (f32[32,512]{1,0:T(8,128)}, f32[32,512]{1,0:T(8,128)S(1)}, u32[]{:S(2)}, u32[]{:S(2)}) collective-permute-start(f32[32,512]{1,0:T(8,128)} %param.3), channel_id=1, source_target_pairs={{0,7},{1,2},{2,5},{3,0},{4,3},{5,6},{6,1},{7,4},{8,15},{9,10},{10,... | collective-permute-start | bytes 196616 | tf_op jit(solution)/shard_map/ppermute | solution.py:367
  13.9 10.7 %collective-permute-start.9 = (f32[32,512]{1,0:T(8,128)}, f32[32,512]{1,0:T(8,128)S(1)}, u32[]{:S(2)}, u32[]{:S(2)}) collective-permute-start(f32[32,512]{1,0:T(8,128)} %param.3), channel_id=1, source_target_pairs={{0,2},{1,7},{2,0},{3,5},{4,6},{5,3},{6,4},{7,1},{8,10},{9,15},{10,... | collective-permute-start | bytes 196616 | tf_op jit(solution)/shard_map/ppermute | solution.py:367
  14.5 1.2 collective-permute-start.7
  53.9 4.0 %collective-permute-start.13 = (f32[16,128]{1,0:T(8,128)S(1)}, f32[16,128]{1,0:T(8,128)S(1)}, u32[]{:S(2)}, u32[]{:S(2)}) collective-permute-start(f32[16,128]{1,0:T(8,128)S(1)} %get-tuple-element.23), channel_id=1, source_target_pairs={{0,7},{1,6},{2,5},{3,4},{4,3},{5,2},{6,1},{7,0},{8,15},{9,14},{10,... | collective-permute-start | bytes 24584 | tf_op jit(solution)/shard_map/ppermute | solution.py:367
  55.1 3.7 %collective-permute-start.12 = (f32[16,128]{1,0:T(8,128)S(1)}, f32[16,128]{1,0:T(8,128)S(1)}, u32[]{:S(2)}, u32[]{:S(2)}) collective-permute-start(f32[16,128]{1,0:T(8,128)S(1)} %get-tuple-element.23), channel_id=1, source_target_pairs={{0,2},{1,3},{2,0},{3,1},{4,6},{5,7},{6,4},{7,5},{8,10},{9,11},{10,... | collective-permute-start | bytes 24584 | tf_op jit(solution)/shard_map/ppermute | solution.py:367
  55.6 3.1 %collective-permute-start.11 = (f32[16,128]{1,0:T(8,128)S(1)}, f32[16,128]{1,0:T(8,128)S(1)}, u32[]{:S(2)}, u32[]{:S(2)}) collective-permute-start(f32[16,128]{1,0:T(8,128)S(1)} %get-tuple-element.23), channel_id=1, source_target_pairs={{0,5},{1,4},{2,7},{3,6},{4,1},{5,0},{6,3},{7,2},{8,13},{9,12},{10,... | collective-permute-start | bytes 24584 | tf_op jit(solution)/shard_map/ppermute | solution.py:367
  81.0 1.2 collective-permute-start.14
  82.3 4.9 %collective-permute-start.17 = (f32[16,128]{1,0:T(8,128)S(1)}, f32[16,128]{1,0:T(8,128)S(1)}, u32[]{:S(2)}, u32[]{:S(2)}) collective-permute-start(f32[16,128]{1,0:T(8,128)S(1)} %multiply_add_fusion.2), channel_id=1, source_target_pairs={{0,28},{4,24},{8,20},{12,16},{16,12},{20,8},{24,4},{28,0},{1,29},{... | collective-permute-start | bytes 24584 | tf_op jit(solution)/shard_map/ppermute | solution.py:357
  85.1 4.0 %collective-permute-start.16 = (f32[16,128]{1,0:T(8,128)S(1)}, f32[16,128]{1,0:T(8,128)S(1)}, u32[]{:S(2)}, u32[]{:S(2)}) collective-permute-start(f32[16,128]{1,0:T(8,128)S(1)} %multiply_add_fusion.2), channel_id=1, source_target_pairs={{0,20},{4,16},{8,28},{12,24},{16,4},{20,0},{24,12},{28,8},{1,21},{... | collective-permute-start | bytes 24584 | tf_op jit(solution)/shard_map/ppermute | solution.py:357
  85.1 4.0 %collective-permute-start.15 = (f32[16,128]{1,0:T(8,128)S(1)}, f32[16,128]{1,0:T(8,128)S(1)}, u32[]{:S(2)}, u32[]{:S(2)}) collective-permute-start(f32[16,128]{1,0:T(8,128)S(1)} %multiply_add_fusion.2), channel_id=1, source_target_pairs={{0,12},{4,8},{8,4},{12,0},{16,28},{20,24},{24,20},{28,16},{1,13},{... | collective-permute-start | bytes 24584 | tf_op jit(solution)/shard_map/ppermute | solution.py:357
  90.3 4.0 %collective-permute-start.20 = (f32[16,128]{1,0:T(8,128)S(1)}, f32[16,128]{1,0:T(8,128)S(1)}, u32[]{:S(2)}, u32[]{:S(2)}) collective-permute-start(f32[16,128]{1,0:T(8,128)S(1)} %get-tuple-element.29), channel_id=1, source_target_pairs={{0,7},{1,6},{2,5},{3,4},{4,3},{5,2},{6,1},{7,0},{8,15},{9,14},{10,... | collective-permute-start | bytes 24584 | tf_op jit(solution)/shard_map/ppermute | solution.py:367
  92.6 3.7 %collective-permute-start.19 = (f32[16,128]{1,0:T(8,128)S(1)}, f32[16,128]{1,0:T(8,128)S(1)}, u32[]{:S(2)}, u32[]{:S(2)}) collective-permute-start(f32[16,128]{1,0:T(8,128)S(1)} %get-tuple-element.29), channel_id=1, source_target_pairs={{0,2},{1,3},{2,0},{3,1},{4,6},{5,7},{6,4},{7,5},{8,10},{9,11},{10,... | collective-permute-start | bytes 24584 | tf_op jit(solution)/shard_map/ppermute | solution.py:367
  93.2 3.1 %collective-permute-start.18 = (f32[16,128]{1,0:T(8,128)S(1)}, f32[16,128]{1,0:T(8,128)S(1)}, u32[]{:S(2)}, u32[]{:S(2)}) collective-permute-start(f32[16,128]{1,0:T(8,128)S(1)} %get-tuple-element.29), channel_id=1, source_target_pairs={{0,5},{1,4},{2,7},{3,6},{4,1},{5,0},{6,3},{7,2},{8,13},{9,12},{10,... | collective-permute-start | bytes 24584 | tf_op jit(solution)/shard_map/ppermute | solution.py:367
  97.5 1.2 collective-permute-start.21
  98.7 4.9 %collective-permute-start.24 = (f32[16,128]{1,0:T(8,128)S(1)}, f32[16,128]{1,0:T(8,128)S(1)}, u32[]{:S(2)}, u32[]{:S(2)}) collective-permute-start(f32[16,128]{1,0:T(8,128)S(1)} %add.120), channel_id=1, source_target_pairs={{0,28},{4,24},{8,20},{12,16},{16,12},{20,8},{24,4},{28,0},{1,29},{... | collective-permute-start | bytes 24584 | tf_op jit(solution)/shard_map/ppermute | solution.py:357
  100.0 4.0 %collective-permute-start.23 = (f32[16,128]{1,0:T(8,128)S(1)}, f32[16,128]{1,0:T(8,128)S(1)}, u32[]{:S(2)}, u32[]{:S(2)}) collective-permute-start(f32[16,128]{1,0:T(8,128)S(1)} %add.120), channel_id=1, source_target_pairs={{0,20},{4,16},{8,28},{12,24},{16,4},{20,0},{24,12},{28,8},{1,21},{... | collective-permute-start | bytes 24584 | tf_op jit(solution)/shard_map/ppermute | solution.py:357
  100.5 3.6 %collective-permute-start.22 = (f32[16,128]{1,0:T(8,128)S(1)}, f32[16,128]{1,0:T(8,128)S(1)}, u32[]{:S(2)}, u32[]{:S(2)}) collective-permute-start(f32[16,128]{1,0:T(8,128)S(1)} %add.120), channel_id=1, source_target_pairs={{0,12},{4,8},{8,4},{12,0},{16,28},{20,24},{24,20},{28,16},{1,13},{... | collective-permute-start | bytes 24584 | tf_op jit(solution)/shard_map/ppermute | solution.py:357
  105.3 4.0 %collective-permute-start.27 = (f32[16,128]{1,0:T(8,128)S(1)}, f32[16,128]{1,0:T(8,128)S(1)}, u32[]{:S(2)}, u32[]{:S(2)}) collective-permute-start(f32[16,128]{1,0:T(8,128)S(1)} %shard_map.55), channel_id=1, source_target_pairs={{0,7},{1,6},{2,5},{3,4},{4,3},{5,2},{6,1},{7,0},{8,15},{9,14},{10,... | collective-permute-start | bytes 24584 | tf_op jit(solution)/shard_map/ppermute | solution.py:367
  106.7 3.7 %collective-permute-start.26 = (f32[16,128]{1,0:T(8,128)S(1)}, f32[16,128]{1,0:T(8,128)S(1)}, u32[]{:S(2)}, u32[]{:S(2)}) collective-permute-start(f32[16,128]{1,0:T(8,128)S(1)} %shard_map.55), channel_id=1, source_target_pairs={{0,2},{1,3},{2,0},{3,1},{4,6},{5,7},{6,4},{7,5},{8,10},{9,11},{10,... | collective-permute-start | bytes 24584 | tf_op jit(solution)/shard_map/ppermute | solution.py:367
  107.3 3.1 %collective-permute-start.25 = (f32[16,128]{1,0:T(8,128)S(1)}, f32[16,128]{1,0:T(8,128)S(1)}, u32[]{:S(2)}, u32[]{:S(2)}) collective-permute-start(f32[16,128]{1,0:T(8,128)S(1)} %shard_map.55), channel_id=1, source_target_pairs={{0,5},{1,4},{2,7},{3,6},{4,1},{5,0},{6,3},{7,2},{8,13},{9,12},{10,... | collective-permute-start | bytes 24584 | tf_op jit(solution)/shard_map/ppermute | solution.py:367
  111.6 1.2 collective-permute-start.28
  112.9 4.9 %collective-permute-start.31 = (f32[16,128]{1,0:T(8,128)S(1)}, f32[16,128]{1,0:T(8,128)S(1)}, u32[]{:S(2)}, u32[]{:S(2)}) collective-permute-start(f32[16,128]{1,0:T(8,128)S(1)} %add.127), channel_id=1, source_target_pairs={{0,28},{4,24},{8,20},{12,16},{16,12},{20,8},{24,4},{28,0},{1,29},{... | collective-permute-start | bytes 24584 | tf_op jit(solution)/shard_map/ppermute | solution.py:357
  115.0 4.0 %collective-permute-start.30 = (f32[16,128]{1,0:T(8,128)S(1)}, f32[16,128]{1,0:T(8,128)S(1)}, u32[]{:S(2)}, u32[]{:S(2)}) collective-permute-start(f32[16,128]{1,0:T(8,128)S(1)} %add.127), channel_id=1, source_target_pairs={{0,20},{4,16},{8,28},{12,24},{16,4},{20,0},{24,12},{28,8},{1,21},{... | collective-permute-start | bytes 24584 | tf_op jit(solution)/shard_map/ppermute | solution.py:357
  115.8 3.2 %collective-permute-start.29 = (f32[16,128]{1,0:T(8,128)S(1)}, f32[16,128]{1,0:T(8,128)S(1)}, u32[]{:S(2)}, u32[]{:S(2)}) collective-permute-start(f32[16,128]{1,0:T(8,128)S(1)} %add.127), channel_id=1, source_target_pairs={{0,12},{4,8},{8,4},{12,0},{16,28},{20,24},{24,20},{28,16},{1,13},{... | collective-permute-start | bytes 24584 | tf_op jit(solution)/shard_map/ppermute | solution.py:357
  119.0 15.2 %copy-start = (f32[2048]{0:T(1024)S(1)}, f32[2048]{0:T(1024)}, u32[]{:S(2)}) copy-start(f32[2048]{0:T(1024)} %param.5) | copy-start | bytes 24580
  120.2 4.0 %collective-permute-start.34 = (f32[16,128]{1,0:T(8,128)S(1)}, f32[16,128]{1,0:T(8,128)S(1)}, u32[]{:S(2)}, u32[]{:S(2)}) collective-permute-start(f32[16,128]{1,0:T(8,128)S(1)} %shard_map.57), channel_id=1, source_target_pairs={{0,7},{1,6},{2,5},{3,4},{4,3},{5,2},{6,1},{7,0},{8,15},{9,14},{10,... | collective-permute-start | bytes 24584 | tf_op jit(solution)/shard_map/ppermute | solution.py:367
  122.4 3.7 %collective-permute-start.33 = (f32[16,128]{1,0:T(8,128)S(1)}, f32[16,128]{1,0:T(8,128)S(1)}, u32[]{:S(2)}, u32[]{:S(2)}) collective-permute-start(f32[16,128]{1,0:T(8,128)S(1)} %shard_map.57), channel_id=1, source_target_pairs={{0,2},{1,3},{2,0},{3,1},{4,6},{5,7},{6,4},{7,5},{8,10},{9,11},{10,... | collective-permute-start | bytes 24584 | tf_op jit(solution)/shard_map/ppermute | solution.py:367
  123.0 3.1 %collective-permute-start.32 = (f32[16,128]{1,0:T(8,128)S(1)}, f32[16,128]{1,0:T(8,128)S(1)}, u32[]{:S(2)}, u32[]{:S(2)}) collective-permute-start(f32[16,128]{1,0:T(8,128)S(1)} %shard_map.57), channel_id=1, source_target_pairs={{0,5},{1,4},{2,7},{3,6},{4,1},{5,0},{6,3},{7,2},{8,13},{9,12},{10,... | collective-permute-start | bytes 24584 | tf_op jit(solution)/shard_map/ppermute | solution.py:367
  127.3 1.2 collective-permute-start.36
  127.5 4.9 %collective-permute-start.35 = (f32[16,128]{1,0:T(8,128)S(1)}, f32[16,128]{1,0:T(8,128)S(1)}, u32[]{:S(2)}, u32[]{:S(2)}) collective-permute-start(f32[16,128]{1,0:T(8,128)S(1)} %multiply_add_fusion), channel_id=1, source_target_pairs={{1,5},{3,7},{5,1},{7,3},{9,13},{11,15},{13,9},{15,11},{17,21},{19,... | collective-permute-start | bytes 24584 | tf_op jit(solution)/shard_map/ppermute | solution.py:367
  128.5 4.9 %collective-permute-start.39 = (f32[16,128]{1,0:T(8,128)S(1)}, f32[16,128]{1,0:T(8,128)S(1)}, u32[]{:S(2)}, u32[]{:S(2)}) collective-permute-start(f32[16,128]{1,0:T(8,128)S(1)} %add.136), channel_id=1, source_target_pairs={{0,28},{4,24},{8,20},{12,16},{16,12},{20,8},{24,4},{28,0},{1,29},{... | collective-permute-start | bytes 24584 | tf_op jit(solution)/shard_map/ppermute | solution.py:357
  129.9 4.1 %collective-permute-start.38 = (f32[16,128]{1,0:T(8,128)S(1)}, f32[16,128]{1,0:T(8,128)S(1)}, u32[]{:S(2)}, u32[]{:S(2)}) collective-permute-start(f32[16,128]{1,0:T(8,128)S(1)} %add.136), channel_id=1, source_target_pairs={{0,20},{4,16},{8,28},{12,24},{16,4},{20,0},{24,12},{28,8},{1,21},{... | collective-permute-start | bytes 24584 | tf_op jit(solution)/shard_map/ppermute | solution.py:357
  130.7 3.3 %collective-permute-start.37 = (f32[16,128]{1,0:T(8,128)S(1)}, f32[16,128]{1,0:T(8,128)S(1)}, u32[]{:S(2)}, u32[]{:S(2)}) collective-permute-start(f32[16,128]{1,0:T(8,128)S(1)} %add.136), channel_id=1, source_target_pairs={{0,12},{4,8},{8,4},{12,0},{16,28},{20,24},{24,20},{28,16},{1,13},{... | collective-permute-start | bytes 24584 | tf_op jit(solution)/shard_map/ppermute | solution.py:357

commit v2 on v1

--- a/solution.py
+++ b/solution.py
@@ -15,7 +15,9 @@
 SUB = 8
 MIB = 1024 * 1024
 TILE = 256
-LIFT = 50.0
+HEAD = 40.0
+ROW_LOW, ROW_HIGH = 2.0**20, 2.0**80
+SCALE_LOW, COLUMN_LOW = 2.0**-60, 2.0**-30
 
 VMEM = pl.BlockSpec(memory_space=pltpu.VMEM)
 HBM = pl.BlockSpec(memory_space=pltpu.HBM)
@@ -109,33 +111,25 @@
         ref[pl.ds(start + k, 1), :] = row[:, k * LANES : (k + 1) * LANES]
 
 
-def guarded_sums(left, right, first, pieces, lse):
-    held = []
-    for start, count, row in pieces:
+def guarded_sums(left, right, pieces, base, lse, ratios):
+    totals = []
+    for start, place, count, row in pieces:
         width = min(TILE, count)
         for t in range(count // width):
             cols = pl.ds(pl.multiple_of(start + t * width, LANES), width)
-            held.append((cols, row + t * (width // LANES)))
-
-    def tile(c, cols):
-        return jnp.dot(left[c * TILE : (c + 1) * TILE, :], right[:, cols], preferred_element_type=jnp.float32)
-
-    peaks = []
-    for cols, _ in held:
-        peak = jnp.max(fold_rows(jnp.maximum, tile(0, cols)), axis=0, keepdims=True)
-        peaks.append(peak)
-    for (cols, _), peak in zip(held, peaks):
-        set_addend(right, first, cols, -peak)
-    totals = []
-    for cols, _ in held:
-        total = None
-        for c in range(left.shape[0] // TILE):
-            part = fold_rows(jnp.add, jnp.exp2(tile(c, cols)))
-            total = part if total is None else total + part
-        totals.append(jnp.sum(total, axis=0, keepdims=True))
-    for (_, row), peak, total in zip(held, peaks, totals):
-        put_rows(lse, row, peak + jnp.log2(total))
-    return jnp.max(tree(jnp.maximum, totals)) < 2.0**100
+            out = pl.ds(pl.multiple_of(place + t * width, LANES), width)
+            total = None
+            for c in range(left.shape[0] // TILE):
+                rows = slice(c * TILE, (c + 1) * TILE)
+                tile = jnp.exp2(jnp.dot(left[rows, :], right[:, cols], preferred_element_type=jnp.float32))
+                ratios[rows, out] = tile
+                part = fold_rows(jnp.add, tile)
+                total = part if total is None else total + part
+            total = jnp.sum(total, axis=0, keepdims=True)
+            put_rows(lse, row + t * (width // LANES), base + jnp.log2(total))
+            totals.append(total)
+    low, high = tree(jnp.minimum, totals), tree(jnp.maximum, totals)
+    return jnp.min(jnp.where((low > ROW_LOW) & (high < ROW_HIGH), 1.0, 0.0)) > 0.5
 
 
 def place_pieces(points, index, pieces):
@@ -145,27 +139,30 @@
         points[:, pl.ds(start, width)] = piece[...]
 
 
-def own_scores_kernel(place, own_tgt, own_g0, src, *refs):
-    lse, norms, left, right, stack, points, acc, held_tgt, g0, sems = refs[-10:]
-    tgt = refs[:-10]
+def own_scores_kernel(place, own_src, own_tgt, own_g0, *refs):
+    lse, norms, left, right, base, flag, ratios, stack, points, acc, held_src, held_tgt, g0, sems = refs[-14:]
+    tgt = refs[:-14]
     copies = [
         pltpu.make_async_copy(source, target, sems.at[k])
-        for k, (source, target) in enumerate(((own_tgt, held_tgt), (own_g0, g0)))
+        for k, (source, target) in enumerate(((own_src, held_src), (own_tgt, held_tgt), (own_g0, g0)))
     ]
     for copy in copies:
         copy.start()
-    depth, width = src.shape
+    for copy in copies:
+        copy.wait()
+    depth, width = held_src.shape
     first = 6 * depth
-    x = src[...]
+    x = held_src[...]
     store_rows(norms, jnp.sum(x * x, axis=0, keepdims=True))
     place_sources(x, right, slice(0, width))
-    for copy in copies:
-        copy.wait()
 
     place_pieces(points, place[1], (held_tgt, *tgt))
     ntgt = left.shape[0]
     y = points[...]
     gamma = ALPHA * (g0[...] - jnp.sum(y * y, axis=0, keepdims=True))
+    top = jnp.max(gamma, axis=1, keepdims=True)
+    base[...] = jnp.broadcast_to(top - HEAD, base.shape)
+    gamma = gamma - top + HEAD
     high, mid, low = split3(y)
     for k, part in enumerate((high, mid, low, high, mid, high)):
         stack[k * depth : (k + 1) * depth, :] = part
@@ -177,16 +174,17 @@
     for c in range(ntgt // TILE):
         left[c * TILE : (c + 1) * TILE, :] = stack[:, c * TILE : (c + 1) * TILE].T
 
-    fine = guarded_sums(left, right, first, [(0, width, 0)], lse)
+    fine = guarded_sums(left, right, [(0, place[0] * width, width, 0)], base[:, :1], lse, ratios)
+    flag[...] = jnp.full(flag.shape, jnp.where(fine, 1.0, 0.0), jnp.float32)
 
     @pl.when(jnp.logical_not(fine))
     def _():
-        store_rows(lse, exact_lse(left, right, first, acc))
-
-
-def scores_kernel(place, left, own_right, own_lse, own_norms, *refs):
-    lse, norms, right, acc = refs[-4:]
-    src = refs[:-4]
+        store_rows(lse, exact_lse(left, right, first, acc) + base[:, :1])
+
+
+def scores_kernel(place, left, own_right, own_lse, own_norms, base, own_flag, _, *refs):
+    lse, norms, right, flag, ratios, acc = refs[-6:]
+    src = refs[:-6]
     depth, width = src[0].shape
     first = 6 * depth
     own = place[0] * width
@@ -199,12 +197,13 @@
         x = piece[...]
         put_rows(norms, row, jnp.sum(x * x, axis=0, keepdims=True))
         place_sources(x, right, pl.ds(pl.multiple_of(start, LANES), width))
-        pieces.append((start, width, row))
-    fine = guarded_sums(left, right, first, pieces, lse)
+        pieces.append((start, start, width, row))
+    fine = guarded_sums(left, right, pieces, base[:, :1], lse, ratios)
+    flag[...] = jnp.where(fine, own_flag[...], 0.0)
 
     @pl.when(jnp.logical_not(fine))
     def _():
-        store_rows(lse, exact_lse(left, right, first, acc))
+        store_rows(lse, exact_lse(left, right, first, acc) + base[:, :1])
 
     for k in range(width // LANES):
         row = pl.ds(place[0] * (width // LANES) + k, 1)
@@ -250,23 +249,35 @@
         out[h * SUB : (h + 1) * SUB, :] = join_chains(chains)
 
 
-def first_columns_kernel(log_ntgt, first, left, _, row_lse, ratios, right, phi, peaks, lse, partial, wide, sums):
+def column_sums(ratios, scale, out):
+    tiles = ratios.shape[1] // LANES
+    scales = jnp.concatenate([jnp.broadcast_to(read_row(scale, k), (SUB, LANES)) for k in range(tiles)], axis=1)
+    for h in range(out.shape[0] // SUB):
+        chains = []
+        for index in range(LANES):
+            rows = slice((h * LANES + index) * SUB, (h * LANES + index + 1) * SUB)
+            value = jnp.sum(ratios[rows, :] * scales, axis=1, keepdims=True)
+            if index % QUARTER == 0:
+                chains.append(jnp.broadcast_to(value, (SUB, LANES)))
+            else:
+                chains[-1] = jnp.where(lane_mask(index), value, chains[-1])
+        out[h * SUB : (h + 1) * SUB, :] = join_chains(chains)
+
+
+def first_columns_kernel(
+    log_ntgt, first, left, base, flag, row_lse, _, __, ratios, right, phi, scale, peaks, lse, partial, wide, sums
+):
     phi[...] = log_ntgt - row_lse[...]
-    for k in range(phi.shape[0]):
-        set_addend(right, first, slice(k * LANES, (k + 1) * LANES), read_row(phi, k) + LIFT)
-    halves = TILE // LANES
-    for t in range(ratios.shape[1] // TILE):
-        for c in range(ratios.shape[0] // TILE):
-            rows = slice(c * TILE, (c + 1) * TILE)
-            tile = jnp.exp2(score_tile(left, right, c, t))
-            ratios[rows, t * TILE : (t + 1) * TILE] = tile
-            part = tree(jnp.add, [tile[:, k * LANES : (k + 1) * LANES] for k in range(halves)])
-            partial[rows, :] = part if t == 0 else partial[rows, :] + part
-    fold_lanes(jnp.sum, partial, sums)
+    scale[...] = jnp.exp2(phi[...] + base[...])
+    column_sums(ratios, scale, sums)
     peaks[...] = jnp.zeros(peaks.shape, jnp.float32)
-
-    @pl.when(jnp.logical_not(jnp.min(sums[...]) >= 2.0**-20))
+    low = jnp.min(jnp.where(flag[...] > 0.5, sums[...], -1.0))
+
+    @pl.when(jnp.logical_not((low >= COLUMN_LOW) & (jnp.min(scale[...]) >= SCALE_LOW)))
     def _():
+        for k in range(phi.shape[0]):
+            set_addend(right, first, slice(k * LANES, (k + 1) * LANES), read_row(phi, k) + base[...])
+        scale[...] = jnp.ones(scale.shape, jnp.float32)
         groups = ratios.shape[0] // SUB
         few = 4
 
@@ -305,10 +316,10 @@
         lax.fori_loop(0, groups // few, ratio_step, 0)
         fold_lanes(jnp.sum, partial, sums)
 
-    lse[...] = peaks[...] + (jnp.log2(sums[...]) - LIFT)
-
-
-def row_sums(ratios, weights, out):
+    lse[...] = peaks[...] + jnp.log2(sums[...])
+
+
+def row_sums(ratios, weights, scale, out):
     count = ratios.shape[1]
     total = jnp.zeros((SUB, count), jnp.float32)
     for h in range(weights.shape[0] // SUB):
@@ -317,71 +328,57 @@
             rows = slice((h * LANES + index) * SUB, (h * LANES + index + 1) * SUB)
             total = total + ratios[rows, :] * jnp.broadcast_to(held[:, index : index + 1], (SUB, count))
     store_rows(out, jnp.sum(total, axis=0, keepdims=True))
-
-
-def first_rows_kernel(log_nsrc, ratios, peaks, col_lse, out, weights, base):
-    shift = log_nsrc - col_lse[...]
-    base[...] = shift
-    weights[...] = jnp.exp2(peaks[...] + (shift - LIFT))
-    row_sums(ratios, weights[...], out)
-
-
-def rows_kernel(nsrc, ratios, weights, total, out):
-    row_sums(ratios, weights[...] * (nsrc / total[...]), out)
-
-
-def columns_kernel(ntgt, ratios, weights, total, out, scale):
-    total = total[...]
-    scale[...] = ntgt / total
-    count = ratios.shape[1]
-    tiles = count // LANES
-    scales = jnp.concatenate([jnp.broadcast_to(read_row(scale, k), (SUB, LANES)) for k in range(tiles)], axis=1)
-    for h in range(out.shape[0] // SUB):
-        chains = []
-        for index in range(LANES):
-            rows = slice((h * LANES + index) * SUB, (h * LANES + index + 1) * SUB)
-            value = jnp.sum(ratios[rows, :] * scales, axis=1, keepdims=True)
-            if index % QUARTER == 0:
-                chains.append(jnp.broadcast_to(value, (SUB, LANES)))
-            else:
-                chains[-1] = jnp.where(lane_mask(index), value, chains[-1])
-        rows = slice(h * SUB, (h + 1) * SUB)
-        out[rows, :] = join_chains(chains) * weights[rows, :]
-
-
-def finish_kernel(log_nsrc, base, total, out):
-    out[...] = (base[...] + (log_nsrc - jnp.log2(total[...]))) * (1.0 / ALPHA)
+    out[...] = out[...] * scale[...]
+
+
+def first_rows_kernel(log_nsrc, ratios, scale, peaks, col_lse, out, weights, shift):
+    shift[...] = log_nsrc - col_lse[...]
+    weights[...] = jnp.exp2(peaks[...] + shift[...])
+    row_sums(ratios, weights[...], scale, out)
+
+
+def rows_kernel(nsrc, ratios, scale, weights, total, out):
+    row_sums(ratios, weights[...] * (nsrc / total[...]), scale, out)
+
+
+def columns_kernel(ntgt, ratios, scale, weights, total, out, held):
+    held[...] = scale[...] * (ntgt / total[...])
+    column_sums(ratios, held, out)
+    out[...] = out[...] * weights[...]
+
+
+def finish_kernel(log_nsrc, shift, total, out):
+    out[...] = (shift[...] + (log_nsrc - jnp.log2(total[...]))) * (1.0 / ALPHA)
 
 
 def swap(value, axis, distance):
     return lax.ppermute(value, axis, [(k, k ^ distance) for k in range(lax.axis_size(axis))])
 
 
-def hop(value, distance, lead, step=1):
+def same_block(value, distance):
     nrows, ncols = lax.axis_size("rows"), lax.axis_size("cols")
-    perm = []
-    for row in range(nrows):
-        for col in range(step - 1, ncols, step):
-            other = col ^ distance
-            perm.append((row * ncols + col, lead(row, col, other) * ncols + other))
+    perm = [
+        (row * ncols + col, (row ^ (distance & 1)) * ncols + (col ^ distance))
+        for row in range(nrows)
+        for col in range(ncols)
+    ]
     return lax.ppermute(value, ("rows", "cols"), perm)
-
-
-def to_block(value, distance, odd=False):
-    return hop(value, distance, lambda row, col, other: row ^ (other & 1), 1 + odd)
-
-
-def same_block(value, distance):
-    return hop(value, distance, lambda row, col, other: row ^ ((col ^ other) & 1))
 
 
 def combine_cols(reduce, value):
     return reduce([value] + [same_block(value, d) for d in range(1, lax.axis_size("cols"))])
 
 
+def add_cores(reduce, value):
+    return reduce([value, swap(value, "rows", 1)])
+
+
+def combine_chips(reduce, value):
+    return reduce([value] + [swap(value, "rows", d) for d in range(3, lax.axis_size("rows"), 2)])
+
+
 def combine_rows(reduce, value):
-    value = reduce([value, swap(value, "rows", 1)])
-    return reduce([value] + [swap(value, "rows", d) for d in range(3, lax.axis_size("rows"), 2)])
+    return combine_chips(reduce, add_cores(reduce, value))
 
 
 def add_all(values):
@@ -433,77 +430,89 @@
         return pltpu.with_memory_space_constraint(value, pltpu.VMEM)
 
     targets = gather_rows(target_points)
-    sources = [to_block(source_points, d) for d in range(ncols)]
+    sources = [same_block(source_points, d) for d in range(1, ncols)]
     place = jnp.stack([lax.axis_index("cols"), lax.axis_index("rows")]).astype(jnp.int32)
     bf16 = jnp.bfloat16
     piece = source_points.shape[1]
     by_piece = jax.ShapeDtypeStruct((piece // LANES, LANES), f32)
-    own_lse, own_norms, left, own_right = call(
+    line = jax.ShapeDtypeStruct((1, LANES), f32)
+    own_lse, own_norms, left, own_right, base, own_flag, ratios = call(
         own_scores_kernel,
-        [by_piece, by_piece, pltpu.VMEM((tgt_count, stack), bf16), pltpu.VMEM((stack, piece), bf16)],
+        [
+            by_piece,
+            by_piece,
+            pltpu.VMEM((tgt_count, stack), bf16),
+            pltpu.VMEM((stack, piece), bf16),
+            line,
+            line,
+            square,
+        ],
         3 + nrows,
         [
             pltpu.VMEM((stack, tgt_count), bf16),
             pltpu.VMEM((depth, tgt_count), f32),
             pltpu.VMEM((SUB, piece), f32),
+            pltpu.VMEM(source_points.shape, f32),
             pltpu.VMEM(target_points.shape, f32),
             pltpu.VMEM((1, tgt_count), f32),
-            pltpu.SemaphoreType.DMA((2,)),
+            pltpu.SemaphoreType.DMA((3,)),
         ],
         limit=16,
         smem=1,
-        hbm=2,
+        hbm=3,
     )(
         place,
         *(
             pltpu.with_memory_space_constraint(own, pltpu.HBM)
-            for own in (target_points, target_init.reshape(1, tgt_count))
+            for own in (source_points, target_points, target_init.reshape(1, tgt_count))
         ),
-        sources[0],
         *targets,
     )
     left = pin(left)
-    lse, norms, right = call(
+    lse, norms, right, flag, ratios = call(
         scores_kernel,
-        [by_src, by_src, pltpu.VMEM((stack, src_count), bf16)],
-        4 + ncols,
+        [by_src, by_src, pltpu.VMEM((stack, src_count), bf16), line, square],
+        7 + ncols,
         [pltpu.VMEM((SUB, src_count), f32)],
         limit=16,
         smem=1,
-    )(place, left, pin(own_right), own_lse, own_norms, *sources[1:])
-    ratios, _, phi, peaks, lse = call(
+        aliases={7: 4},
+    )(place, left, pin(own_right), own_lse, own_norms, base, own_flag, pin(ratios), *sources)
+    ratios, _, phi, scale, peaks, lse = call(
         functools.partial(first_columns_kernel, log_ntgt, 6 * depth),
-        [square, pltpu.VMEM((stack, src_count), jnp.bfloat16), by_src, by_tgt, by_tgt],
-        3,
+        [square, pltpu.VMEM((stack, src_count), bf16), by_src, by_src, by_tgt, by_tgt],
+        6,
         [wide, wide, row_tgt],
-        aliases={1: 1},
-    )(left, pin(right), combine_cols(lse2, lse))
+        aliases={4: 0, 5: 1},
+    )(left, base, flag, combine_cols(lse2, lse), pin(ratios), pin(right))
     ratios = pin(ratios)
-    total, weights, base = call(
+    total, weights, shift = call(
         functools.partial(first_rows_kernel, log_nsrc),
         [by_src, by_tgt, by_tgt],
-        3,
-    )(ratios, peaks, combine_rows(lse2, lse))
+        4,
+    )(ratios, scale, peaks, combine_rows(lse2, lse))
     for step in range(1, ITERS):
         row_total = combine_cols(add_all, total)
         (total,) = call(
             functools.partial(columns_kernel, float(ntgt)),
             [by_tgt],
-            3,
+            4,
             [row_src],
-        )(ratios, weights, row_total)
+        )(ratios, scale, weights, row_total)
+        total = add_cores(add_all, total)
         if step == ITERS - 1:
             total, row_total = lax.optimization_barrier((total, row_total))
-        total = combine_rows(add_all, total)
+        total = combine_chips(add_all, total)
         if step < ITERS - 1:
             (total,) = call(
                 functools.partial(rows_kernel, float(nsrc)),
                 [by_src],
-                3,
-            )(ratios, weights, total)
+                4,
+            )(ratios, scale, weights, total)
     f = (phi + (log_ntgt - jnp.log2(row_total))) * (1.0 / ALPHA) + norms
-    f = jnp.where(lax.axis_index("cols") % 2 == 1, to_block(f, 0, odd=True), f)
-    (delta,) = call(functools.partial(finish_kernel, log_nsrc), [by_tgt], 2)(base, total)
+    column = lax.broadcasted_iota(jnp.int32, f.shape, 0) // (piece // LANES)
+    f = jnp.where((column - lax.axis_index("cols")) % 2 == 0, f, swap(f, "rows", 1))
+    (delta,) = call(functools.partial(finish_kernel, log_nsrc), [by_tgt], 2)(shift, total)
     delta = delta.reshape(-1, SUB, LANES).transpose(0, 2, 1).reshape(-1)
     return f.reshape(-1), target_init + delta
 

time: 135 us -> 133 us (0.985)
  Pallas kernels: 67.7 us -> 66.3 us
    pallas_call x1, Pallas kernels: 22.3 us -> 20.9 us  [body(): call(functools.partial(first_columns_kernel, log_ntgt, 6 * depth), [squar...]
    ppermute x23 -> x24, waiting for transfers between devices: 14 us -> 14.7 us  [swap(): lax.ppermute(value, axis, [(k, k ^ distance) for k in range(lax.axis_size...]
    ppermute x17 -> x15, starting transfers between devices: 18.3 us -> 17.6 us  [same_block(): return lax.ppermute(value, ('rows', 'cols'), perm)]
    ppermute x23 -> x24, starting transfers between devices: 22.5 us -> 21.9 us  [swap(): lax.ppermute(value, axis, [(k, k ^ distance) for k in range(lax.axis_size...]
    ppermute x17 -> x15, waiting for transfers between devices: 9.86 us -> 9.25 us  [same_block(): return lax.ppermute(value, ('rows', 'cols'), perm)]
  transfers between devices with their start and end apart: 40 -> 39, of which waited for: 26 -> 24; matrix products, arithmetic and copies ran while one was open for 1% -> 1% of each run, Pallas kernels for 7% -> 7%
where the time goes in v2:
time: 133 us; the launch traced here: 132 us
  Pallas kernels  66.3 us (50%)
  starting transfers between devices  39.5 us (30%)
  waiting for transfers between devices  24 us (18%)
  other arithmetic  1.49 us (1%)
    pallas_call x1, Pallas kernels, body(): call(scores_kernel, [by_src, by_src, pltpu.VMEM((stack, src_count), bf16)...  28.9 us
    ppermute x24, starting transfers between devices, swap(): lax.ppermute(value, axis, [(k, k ^ distance) for k in range(lax.axis_size...  21.9 us
    pallas_call x1, Pallas kernels, body(): call(functools.partial(first_columns_kernel, log_ntgt, 6 * depth), [squar...  20.9 us
    ppermute x15, starting transfers between devices, same_block(): return lax.ppermute(value, ('rows', 'cols'), perm)  17.6 us
    ppermute x24, waiting for transfers between devices, swap(): lax.ppermute(value, axis, [(k, k ^ distance) for k in range(lax.axis_size...  14.7 us
    ppermute x15, waiting for transfers between devices, same_block(): return lax.ppermute(value, ('rows', 'cols'), perm)  9.25 us
    pallas_call x1, Pallas kernels, body(): call(own_scores_kernel, [by_piece, by_piece, pltpu.VMEM((tgt_count, stack...  8.94 us
    pallas_call x3, Pallas kernels, body(): call(functools.partial(columns_kernel, float(ntgt)), [by_tgt], 4, [row_src])  3.98 us
  transfers between devices with their start and end apart: 39, of which 24 were waited for; matrix products, arithmetic and copies ran while one was open for 1% of the time, Pallas kernels for 7%

profile of v2, /device:TPU:0, one launch (start us, length us, event | category | flops | bytes accessed | tf_op | source)
XLA Modules:
  0.0 132.4 jit_solution(11824013064919357809)
XLA Ops:
  0.6 2.5 %collective-permute-start.1 = (f32[32,256]{1,0:T(8,128)}, f32[32,256]{1,0:T(8,128)S(1)}, u32[]{:S(2)}, u32[]{:S(2)}) collective-permute-start(f32[32,256]{1,0:T(8,128)} %own_tgt.1), channel_id=1, source_target_pairs={{0,12},{4,8},{8,4},{12,0},{16,28},{20,24},{24,20},{28,16},{1,13},{... | collective-permute-start | bytes 98312 | tf_op jit(solution)/shard_map/ppermute | solution.py:355
  3.2 0.7 collective-permute-start
  3.8 2.2 %collective-permute-start.3 = (f32[32,256]{1,0:T(8,128)}, f32[32,256]{1,0:T(8,128)S(1)}, u32[]{:S(2)}, u32[]{:S(2)}) collective-permute-start(f32[32,256]{1,0:T(8,128)} %own_tgt.1), channel_id=1, source_target_pairs={{0,20},{4,16},{8,28},{12,24},{16,4},{20,0},{24,12},{28,8},{1,21},{... | collective-permute-start | bytes 98312 | tf_op jit(solution)/shard_map/ppermute | solution.py:355
  6.5 1.4 %collective-permute-start.7 = (f32[32,512]{1,0:T(8,128)}, f32[32,512]{1,0:T(8,128)S(1)}, u32[]{:S(2)}, u32[]{:S(2)}) collective-permute-start(f32[32,512]{1,0:T(8,128)} %own_src.1), channel_id=1, source_target_pairs={{0,5},{1,4},{2,7},{3,6},{4,1},{5,0},{6,3},{7,2},{8,13},{9,12},{10,... | collective-permute-start | bytes 196616 | tf_op jit(solution)/shard_map/ppermute | solution.py:365
  8.0 1.5 %collective-permute-start.8 = (f32[32,512]{1,0:T(8,128)}, f32[32,512]{1,0:T(8,128)S(1)}, u32[]{:S(2)}, u32[]{:S(2)}) collective-permute-start(f32[32,512]{1,0:T(8,128)} %own_src.1), channel_id=1, source_target_pairs={{0,2},{1,3},{2,0},{3,1},{4,6},{5,7},{6,4},{7,5},{8,10},{9,11},{10,... | collective-permute-start | bytes 196616 | tf_op jit(solution)/shard_map/ppermute | solution.py:365
  9.5 1.9 %collective-permute-start.9 = (f32[32,512]{1,0:T(8,128)}, f32[32,512]{1,0:T(8,128)S(1)}, u32[]{:S(2)}, u32[]{:S(2)}) collective-permute-start(f32[32,512]{1,0:T(8,128)} %own_src.1), channel_id=1, source_target_pairs={{0,7},{1,6},{2,5},{3,4},{4,3},{5,2},{6,1},{7,0},{8,15},{9,14},{10,... | collective-permute-start | bytes 196616 | tf_op jit(solution)/shard_map/ppermute | solution.py:365
  12.0 0.8 collective-permute-done.4.refs_3_
  13.1 8.9 %shard_map.50 = (f32[4,128]{1,0:T(4,128)S(1)}, f32[4,128]{1,0:T(4,128)S(1)}, bf16[2048,256]{1,0:T(8,128)(2,1)S(1)}, bf16[256,512]{1,0:T(8,128)(2,1)S(1)}, f32[1,...) custom-call(s32[2]{0:T(128)S(1)} %pad_add_fusion.place, f32[32,512]{1,0:T(8,128)} %own_src.1, ...), custom_call_target="tpu_custom_call" | custom-call | tf_op jit(solution)/shard_map/pallas_call | solution.py:439
  22.1 28.9 %shard_map.51 = (f32[16,128]{1,0:T(8,128)S(1)}, f32[16,128]{1,0:T(8,128)S(1)}, bf16[256,2048]{1,0:T(8,128)(2,1)S(1)}, f32[1,128]{1,0:T(1,128)S(1)}, f32[2048,2048]{1,0:T(8,128)S(1)}) custom-call(s32[2]{0:T(128)S(1)} %pad_add_fusion.place, bf16[2048,256]{1,0:T(8,128)(2,1)S(1)} %get-tuple-element.24.left, ...), custom_call_target="tpu_custom_call", output_to_operand_aliasing={{4}: (7, {})} | custom-call | tf_op jit(solution)/shard_map/pallas_call | solution.py:472
  51.0 2.3 %collective-permute-start.12 = (f32[16,128]{1,0:T(8,128)S(1)}, f32[16,128]{1,0:T(8,128)S(1)}, u32[]{:S(2)}, u32[]{:S(2)}) collective-permute-start(f32[16,128]{1,0:T(8,128)S(1)} %get-tuple-element.32), channel_id=1, source_target_pairs={{0,7},{1,6},{2,5},{3,4},{4,3},{5,2},{6,1},{7,0},{8,15},{9,14},{10,... | collective-permute-start | bytes 24584 | tf_op jit(solution)/shard_map/ppermute | solution.py:365
  54.0 1.0 collective-permute-done.12
  55.0 1.9 %collective-permute-done.11 = f32[16,128]{1,0:T(8,128)S(1)} collective-permute-done((f32[16,128]{1,0:T(8,128)S(1)}, f32[16,128]{1,0:T(8,128)S(1)}, u32[]{:S(2)}, u32[]{:S(2)}) %collective-permute-start.11) | collective-permute-done | bytes 8224 | tf_op jit(solution)/shard_map/ppermute | solution.py:365
  57.0 20.9 %shard_map.52 = (f32[2048,2048]{1,0:T(8,128)S(1)}, bf16[256,2048]{1,0:T(8,128)(2,1)S(1)}, f32[16,128]{1,0:T(8,128)S(1)}, f32[16,128]{1,0:T(8,128)S(1)}, f32[16,128]{1,0:T(8,128)S(1)}, /*index=5*/f32[16,128]{1,0:T(8,128)S(1)}) custom-call(bf16[2048,256]{1,0:T(8,128)(2,1)S(1)} %get-tuple-element.24.left, ...), custom_call_target="tpu_custom_call", output_to_operand_aliasing={{0}: (4, {}), {1}: (5, {})} | custom-call | tf_op jit(solution)/shard_map/pallas_call | solution.py:481
  78.0 1.1 collective-permute-done.13
  79.1 1.7 %collective-permute-start.16 = (f32[16,128]{1,0:T(8,128)S(1)}, f32[16,128]{1,0:T(8,128)S(1)}, u32[]{:S(2)}, u32[]{:S(2)}) collective-permute-start(f32[16,128]{1,0:T(8,128)S(1)} %multiply_add_fusion.2), channel_id=1, source_target_pairs={{0,28},{4,24},{8,20},{12,16},{16,12},{20,8},{24,4},{28,0},{1,29},{... | collective-permute-start | bytes 24584 | tf_op jit(solution)/shard_map/ppermute | solution.py:355
  80.8 2.3 %collective-permute-start.14 = (f32[16,128]{1,0:T(8,128)S(1)}, f32[16,128]{1,0:T(8,128)S(1)}, u32[]{:S(2)}, u32[]{:S(2)}) collective-permute-start(f32[16,128]{1,0:T(8,128)S(1)} %multiply_add_fusion.2), channel_id=1, source_target_pairs={{0,12},{4,8},{8,4},{12,0},{16,28},{20,24},{24,20},{28,16},{1,13},{... | collective-permute-start | bytes 24584 | tf_op jit(solution)/shard_map/ppermute | solution.py:355
  83.0 1.0 collective-permute-done.16
  84.0 0.7 collective-permute-done.15
  84.8 1.2 shard_map.53
  86.0 1.5 %collective-permute-start.18 = (f32[16,128]{1,0:T(8,128)S(1)}, f32[16,128]{1,0:T(8,128)S(1)}, u32[]{:S(2)}, u32[]{:S(2)}) collective-permute-start(f32[16,128]{1,0:T(8,128)S(1)} %get-tuple-element.41), channel_id=1, source_target_pairs={{0,2},{1,3},{2,0},{3,1},{4,6},{5,7},{6,4},{7,5},{8,10},{9,11},{10,... | collective-permute-start | bytes 24584 | tf_op jit(solution)/shard_map/ppermute | solution.py:365
  87.8 1.5 %collective-permute-start.17 = (f32[16,128]{1,0:T(8,128)S(1)}, f32[16,128]{1,0:T(8,128)S(1)}, u32[]{:S(2)}, u32[]{:S(2)}) collective-permute-start(f32[16,128]{1,0:T(8,128)S(1)} %get-tuple-element.41), channel_id=1, source_target_pairs={{0,5},{1,4},{2,7},{3,6},{4,1},{5,0},{6,3},{7,2},{8,13},{9,12},{10,... | collective-permute-start | bytes 24584 | tf_op jit(solution)/shard_map/ppermute | solution.py:365
  89.7 1.8 %collective-permute-done.19 = f32[16,128]{1,0:T(8,128)S(1)} collective-permute-done((f32[16,128]{1,0:T(8,128)S(1)}, f32[16,128]{1,0:T(8,128)S(1)}, u32[]{:S(2)}, u32[]{:S(2)}) %collective-permute-start.19) | collective-permute-done | bytes 8224 | tf_op jit(solution)/shard_map/ppermute | solution.py:365
  91.5 1.3 %shard_map.54 = f32[16,128]{1,0:T(8,128)S(1)} custom-call(f32[2048,2048]{1,0:T(8,128)S(1)} %get-tuple-element.36.ratios, f32[16,128]{1,0:T(8,128)S(1)} %get-tuple-element.37.scale, f32[16,128]{1,0:T(8,128)S(1)} %get-tuple-element.40.weights, f32[16,128]{1,0:T(8,128)S(1)} %add_add_fusion.5.total), custom_call_target="tpu_custom_call" | custom-call | tf_op jit(solution)/shard_map/pallas_call | solution.py:496
  93.0 1.0 collective-permute-done.20
  94.0 1.8 %collective-permute-start.22 = (f32[16,128]{1,0:T(8,128)S(1)}, f32[16,128]{1,0:T(8,128)S(1)}, u32[]{:S(2)}, u32[]{:S(2)}) collective-permute-start(f32[16,128]{1,0:T(8,128)S(1)} %add.124), channel_id=1, source_target_pairs={{0,20},{4,16},{8,28},{12,24},{16,4},{20,0},{24,12},{28,8},{1,21},{... | collective-permute-start | bytes 24584 | tf_op jit(solution)/shard_map/ppermute | solution.py:355
  95.8 2.0 %collective-permute-start.23 = (f32[16,128]{1,0:T(8,128)S(1)}, f32[16,128]{1,0:T(8,128)S(1)}, u32[]{:S(2)}, u32[]{:S(2)}) collective-permute-start(f32[16,128]{1,0:T(8,128)S(1)} %add.124), channel_id=1, source_target_pairs={{0,28},{4,24},{8,20},{12,16},{16,12},{20,8},{24,4},{28,0},{1,29},{... | collective-permute-start | bytes 24584 | tf_op jit(solution)/shard_map/ppermute | solution.py:355
  98.0 2.7 %collective-permute-done.23 = f32[16,128]{1,0:T(8,128)S(1)} collective-permute-done((f32[16,128]{1,0:T(8,128)S(1)}, f32[16,128]{1,0:T(8,128)S(1)}, u32[]{:S(2)}, u32[]{:S(2)}) %collective-permute-start.23) | collective-permute-done | bytes 8224 | tf_op jit(solution)/shard_map/ppermute | solution.py:355
  100.8 1.2 shard_map.55
  102.0 1.0 collective-permute-start.25
  103.0 1.1 collective-permute-start.26
  104.1 1.2 collective-permute-start.24
  105.7 1.3 collective-permute-done.26
  107.2 1.3 %shard_map.56 = f32[16,128]{1,0:T(8,128)S(1)} custom-call(f32[2048,2048]{1,0:T(8,128)S(1)} %get-tuple-element.36.ratios, f32[16,128]{1,0:T(8,128)S(1)} %get-tuple-element.37.scale, f32[16,128]{1,0:T(8,128)S(1)} %get-tuple-element.40.weights, f32[16,128]{1,0:T(8,128)S(1)} %add_add_fusion.3.total), custom_call_target="tpu_custom_call" | custom-call | tf_op jit(solution)/shard_map/pallas_call | solution.py:496
  109.1 0.8 collective-permute-done.27
  110.5 1.8 %collective-permute-start.30 = (f32[16,128]{1,0:T(8,128)S(1)}, f32[16,128]{1,0:T(8,128)S(1)}, u32[]{:S(2)}, u32[]{:S(2)}) collective-permute-start(f32[16,128]{1,0:T(8,128)S(1)} %add.131), channel_id=1, source_target_pairs={{0,28},{4,24},{8,20},{12,16},{16,12},{20,8},{24,4},{28,0},{1,29},{... | collective-permute-start | bytes 24584 | tf_op jit(solution)/shard_map/ppermute | solution.py:355
  112.2 0.9 collective-permute-start.28
  113.1 0.8 collective-permute-done.29
  113.9 1.5 %collective-permute-done.30 = f32[16,128]{1,0:T(8,128)S(1)} collective-permute-done((f32[16,128]{1,0:T(8,128)S(1)}, f32[16,128]{1,0:T(8,128)S(1)}, u32[]{:S(2)}, u32[]{:S(2)}) %collective-permute-start.30) | collective-permute-done | bytes 8224 | tf_op jit(solution)/shard_map/ppermute | solution.py:355
  115.4 1.2 shard_map.57
  116.6 1.5 %collective-permute-start.32 = (f32[16,128]{1,0:T(8,128)S(1)}, f32[16,128]{1,0:T(8,128)S(1)}, u32[]{:S(2)}, u32[]{:S(2)}) collective-permute-start(f32[16,128]{1,0:T(8,128)S(1)} %shard_map.57), channel_id=1, source_target_pairs={{0,2},{1,3},{2,0},{3,1},{4,6},{5,7},{6,4},{7,5},{8,10},{9,11},{10,... | collective-permute-start | bytes 24584 | tf_op jit(solution)/shard_map/ppermute | solution.py:365
  118.8 1.1 collective-permute-start.31
  120.4 1.8 %collective-permute-done.33 = f32[16,128]{1,0:T(8,128)S(1)} collective-permute-done((f32[16,128]{1,0:T(8,128)S(1)}, f32[16,128]{1,0:T(8,128)S(1)}, u32[]{:S(2)}, u32[]{:S(2)}) %collective-permute-start.33) | collective-permute-done | bytes 8224 | tf_op jit(solution)/shard_map/ppermute | solution.py:365
  122.1 1.3 %shard_map.58 = f32[16,128]{1,0:T(8,128)S(1)} custom-call(f32[2048,2048]{1,0:T(8,128)S(1)} %get-tuple-element.36.ratios, f32[16,128]{1,0:T(8,128)S(1)} %get-tuple-element.37.scale, f32[16,128]{1,0:T(8,128)S(1)} %get-tuple-element.40.weights, f32[16,128]{1,0:T(8,128)S(1)} %add_add_fusion.1.total), custom_call_target="tpu_custom_call" | custom-call | tf_op jit(solution)/shard_map/pallas_call | solution.py:496
  123.8 0.9 collective-permute-done.34
  124.7 1.2 collective-permute-start.37
  125.9 1.7 %collective-permute-start.38 = (f32[16,128]{1,0:T(8,128)S(1)}, f32[16,128]{1,0:T(8,128)S(1)}, u32[]{:S(2)}, u32[]{:S(2)}) collective-permute-start(f32[16,128]{1,0:T(8,128)S(1)} %add.138), channel_id=1, source_target_pairs={{0,28},{4,24},{8,20},{12,16},{16,12},{20,8},{24,4},{28,0},{1,29},{... | collective-permute-start | bytes 24584 | tf_op jit(solution)/shard_map/ppermute | solution.py:355
  128.7 2.1 %collective-permute-done.38 = f32[16,128]{1,0:T(8,128)S(1)} collective-permute-done((f32[16,128]{1,0:T(8,128)S(1)}, f32[16,128]{1,0:T(8,128)S(1)}, u32[]{:S(2)}, u32[]{:S(2)}) %collective-permute-start.38) | collective-permute-done | bytes 8224 | tf_op jit(solution)/shard_map/ppermute | solution.py:355
  131.7 0.7 select_bitcast_fusion
  (62 shorter events, 8.8 us)
Async XLA Ops:
  0.6 5.4 %collective-permute-start.1 = (f32[32,256]{1,0:T(8,128)}, f32[32,256]{1,0:T(8,128)S(1)}, u32[]{:S(2)}, u32[]{:S(2)}) collective-permute-start(f32[32,256]{1,0:T(8,128)} %own_tgt.1), channel_id=1, source_target_pairs={{0,12},{4,8},{8,4},{12,0},{16,28},{20,24},{24,20},{28,16},{1,13},{... | collective-permute-start | bytes 98312 | tf_op jit(solution)/shard_map/ppermute | solution.py:355
  3.2 4.8 %collective-permute-start = (f32[32,256]{1,0:T(8,128)}, f32[32,256]{1,0:T(8,128)S(1)}, u32[]{:S(2)}, u32[]{:S(2)}) collective-permute-start(f32[32,256]{1,0:T(8,128)} %own_tgt.1), channel_id=1, source_target_pairs={{0,4},{4,0},{8,12},{12,8},{16,20},{20,16},{24,28},{28,24},{1,5},{5... | collective-permute-start | bytes 98312 | tf_op jit(solution)/shard_map/ppermute | solution.py:355
  3.8 5.7 %collective-permute-start.3 = (f32[32,256]{1,0:T(8,128)}, f32[32,256]{1,0:T(8,128)S(1)}, u32[]{:S(2)}, u32[]{:S(2)}) collective-permute-start(f32[32,256]{1,0:T(8,128)} %own_tgt.1), channel_id=1, source_target_pairs={{0,20},{4,16},{8,28},{12,24},{16,4},{20,0},{24,12},{28,8},{1,21},{... | collective-permute-start | bytes 98312 | tf_op jit(solution)/shard_map/ppermute | solution.py:355
  6.0 5.3 %collective-permute-start.5 = (f32[32,256]{1,0:T(8,128)}, f32[32,256]{1,0:T(8,128)S(1)}, u32[]{:S(2)}, u32[]{:S(2)}) collective-permute-start(f32[32,256]{1,0:T(8,128)} %own_tgt.1), channel_id=1, source_target_pairs={{0,28},{4,24},{8,20},{12,16},{16,12},{20,8},{24,4},{28,0},{1,29},{... | collective-permute-start | bytes 98312 | tf_op jit(solution)/shard_map/ppermute | solution.py:355
  6.0 5.9 %collective-permute-start.2 = (f32[32,256]{1,0:T(8,128)S(1)}, f32[32,256]{1,0:T(8,128)S(1)}, u32[]{:S(2)}, u32[]{:S(2)}) collective-permute-start(f32[32,256]{1,0:T(8,128)S(1)} %collective-permute-done.1.refs_2_), channel_id=1, source_target_pairs={{0,4},{4,0},{8,12},{12,8},{16,20},{20,16},{24,28},{28,24},{1,5},{5... | collective-permute-start | bytes 98312 | tf_op jit(solution)/shard_map/ppermute | solution.py:355
  6.5 15.5 %collective-permute-start.7 = (f32[32,512]{1,0:T(8,128)}, f32[32,512]{1,0:T(8,128)S(1)}, u32[]{:S(2)}, u32[]{:S(2)}) collective-permute-start(f32[32,512]{1,0:T(8,128)} %own_src.1), channel_id=1, source_target_pairs={{0,5},{1,4},{2,7},{3,6},{4,1},{5,0},{6,3},{7,2},{8,13},{9,12},{10,... | collective-permute-start | bytes 196616 | tf_op jit(solution)/shard_map/ppermute | solution.py:365
  8.0 14.1 %collective-permute-start.8 = (f32[32,512]{1,0:T(8,128)}, f32[32,512]{1,0:T(8,128)S(1)}, u32[]{:S(2)}, u32[]{:S(2)}) collective-permute-start(f32[32,512]{1,0:T(8,128)} %own_src.1), channel_id=1, source_target_pairs={{0,2},{1,3},{2,0},{3,1},{4,6},{5,7},{6,4},{7,5},{8,10},{9,11},{10,... | collective-permute-start | bytes 196616 | tf_op jit(solution)/shard_map/ppermute | solution.py:365
  9.5 12.6 %collective-permute-start.9 = (f32[32,512]{1,0:T(8,128)}, f32[32,512]{1,0:T(8,128)S(1)}, u32[]{:S(2)}, u32[]{:S(2)}) collective-permute-start(f32[32,512]{1,0:T(8,128)} %own_src.1), channel_id=1, source_target_pairs={{0,7},{1,6},{2,5},{3,4},{4,3},{5,2},{6,1},{7,0},{8,15},{9,14},{10,... | collective-permute-start | bytes 196616 | tf_op jit(solution)/shard_map/ppermute | solution.py:365
  11.4 1.4 %collective-permute-start.4 = (f32[32,256]{1,0:T(8,128)S(1)}, f32[32,256]{1,0:T(8,128)S(1)}, u32[]{:S(2)}, u32[]{:S(2)}) collective-permute-start(f32[32,256]{1,0:T(8,128)S(1)} %collective-permute-done.3.refs_4_), channel_id=1, source_target_pairs={{0,4},{4,0},{8,12},{12,8},{16,20},{20,16},{24,28},{28,24},{1,5},{5... | collective-permute-start | bytes 98312 | tf_op jit(solution)/shard_map/ppermute | solution.py:355
  11.9 1.2 collective-permute-start.6
  51.0 4.0 %collective-permute-start.12 = (f32[16,128]{1,0:T(8,128)S(1)}, f32[16,128]{1,0:T(8,128)S(1)}, u32[]{:S(2)}, u32[]{:S(2)}) collective-permute-start(f32[16,128]{1,0:T(8,128)S(1)} %get-tuple-element.32), channel_id=1, source_target_pairs={{0,7},{1,6},{2,5},{3,4},{4,3},{5,2},{6,1},{7,0},{8,15},{9,14},{10,... | collective-permute-start | bytes 24584 | tf_op jit(solution)/shard_map/ppermute | solution.py:365
  53.3 3.7 %collective-permute-start.11 = (f32[16,128]{1,0:T(8,128)S(1)}, f32[16,128]{1,0:T(8,128)S(1)}, u32[]{:S(2)}, u32[]{:S(2)}) collective-permute-start(f32[16,128]{1,0:T(8,128)S(1)} %get-tuple-element.32), channel_id=1, source_target_pairs={{0,2},{1,3},{2,0},{3,1},{4,6},{5,7},{6,4},{7,5},{8,10},{9,11},{10,... | collective-permute-start | bytes 24584 | tf_op jit(solution)/shard_map/ppermute | solution.py:365
  53.8 3.1 %collective-permute-start.10 = (f32[16,128]{1,0:T(8,128)S(1)}, f32[16,128]{1,0:T(8,128)S(1)}, u32[]{:S(2)}, u32[]{:S(2)}) collective-permute-start(f32[16,128]{1,0:T(8,128)S(1)} %get-tuple-element.32), channel_id=1, source_target_pairs={{0,5},{1,4},{2,7},{3,6},{4,1},{5,0},{6,3},{7,2},{8,13},{9,12},{10,... | collective-permute-start | bytes 24584 | tf_op jit(solution)/shard_map/ppermute | solution.py:365
  77.8 1.2 collective-permute-start.13
  79.1 4.9 %collective-permute-start.16 = (f32[16,128]{1,0:T(8,128)S(1)}, f32[16,128]{1,0:T(8,128)S(1)}, u32[]{:S(2)}, u32[]{:S(2)}) collective-permute-start(f32[16,128]{1,0:T(8,128)S(1)} %multiply_add_fusion.2), channel_id=1, source_target_pairs={{0,28},{4,24},{8,20},{12,16},{16,12},{20,8},{24,4},{28,0},{1,29},{... | collective-permute-start | bytes 24584 | tf_op jit(solution)/shard_map/ppermute | solution.py:355
  80.8 4.0 %collective-permute-start.15 = (f32[16,128]{1,0:T(8,128)S(1)}, f32[16,128]{1,0:T(8,128)S(1)}, u32[]{:S(2)}, u32[]{:S(2)}) collective-permute-start(f32[16,128]{1,0:T(8,128)S(1)} %multiply_add_fusion.2), channel_id=1, source_target_pairs={{0,20},{4,16},{8,28},{12,24},{16,4},{20,0},{24,12},{28,8},{1,21},{... | collective-permute-start | bytes 24584 | tf_op jit(solution)/shard_map/ppermute | solution.py:355
  80.8 4.0 %collective-permute-start.14 = (f32[16,128]{1,0:T(8,128)S(1)}, f32[16,128]{1,0:T(8,128)S(1)}, u32[]{:S(2)}, u32[]{:S(2)}) collective-permute-start(f32[16,128]{1,0:T(8,128)S(1)} %multiply_add_fusion.2), channel_id=1, source_target_pairs={{0,12},{4,8},{8,4},{12,0},{16,28},{20,24},{24,20},{28,16},{1,13},{... | collective-permute-start | bytes 24584 | tf_op jit(solution)/shard_map/ppermute | solution.py:355
  86.0 3.7 %collective-permute-start.18 = (f32[16,128]{1,0:T(8,128)S(1)}, f32[16,128]{1,0:T(8,128)S(1)}, u32[]{:S(2)}, u32[]{:S(2)}) collective-permute-start(f32[16,128]{1,0:T(8,128)S(1)} %get-tuple-element.41), channel_id=1, source_target_pairs={{0,2},{1,3},{2,0},{3,1},{4,6},{5,7},{6,4},{7,5},{8,10},{9,11},{10,... | collective-permute-start | bytes 24584 | tf_op jit(solution)/shard_map/ppermute | solution.py:365
  87.5 4.0 %collective-permute-start.19 = (f32[16,128]{1,0:T(8,128)S(1)}, f32[16,128]{1,0:T(8,128)S(1)}, u32[]{:S(2)}, u32[]{:S(2)}) collective-permute-start(f32[16,128]{1,0:T(8,128)S(1)} %get-tuple-element.41), channel_id=1, source_target_pairs={{0,7},{1,6},{2,5},{3,4},{4,3},{5,2},{6,1},{7,0},{8,15},{9,14},{10,... | collective-permute-start | bytes 24584 | tf_op jit(solution)/shard_map/ppermute | solution.py:365
  87.8 3.7 %collective-permute-start.17 = (f32[16,128]{1,0:T(8,128)S(1)}, f32[16,128]{1,0:T(8,128)S(1)}, u32[]{:S(2)}, u32[]{:S(2)}) collective-permute-start(f32[16,128]{1,0:T(8,128)S(1)} %get-tuple-element.41), channel_id=1, source_target_pairs={{0,5},{1,4},{2,7},{3,6},{4,1},{5,0},{6,3},{7,2},{8,13},{9,12},{10,... | collective-permute-start | bytes 24584 | tf_op jit(solution)/shard_map/ppermute | solution.py:365
  92.8 1.2 collective-permute-start.20
  94.0 4.0 %collective-permute-start.22 = (f32[16,128]{1,0:T(8,128)S(1)}, f32[16,128]{1,0:T(8,128)S(1)}, u32[]{:S(2)}, u32[]{:S(2)}) collective-permute-start(f32[16,128]{1,0:T(8,128)S(1)} %add.124), channel_id=1, source_target_pairs={{0,20},{4,16},{8,28},{12,24},{16,4},{20,0},{24,12},{28,8},{1,21},{... | collective-permute-start | bytes 24584 | tf_op jit(solution)/shard_map/ppermute | solution.py:355
  95.8 4.9 %collective-permute-start.23 = (f32[16,128]{1,0:T(8,128)S(1)}, f32[16,128]{1,0:T(8,128)S(1)}, u32[]{:S(2)}, u32[]{:S(2)}) collective-permute-start(f32[16,128]{1,0:T(8,128)S(1)} %add.124), channel_id=1, source_target_pairs={{0,28},{4,24},{8,20},{12,16},{16,12},{20,8},{24,4},{28,0},{1,29},{... | collective-permute-start | bytes 24584 | tf_op jit(solution)/shard_map/ppermute | solution.py:355
  97.7 3.1 %collective-permute-start.21 = (f32[16,128]{1,0:T(8,128)S(1)}, f32[16,128]{1,0:T(8,128)S(1)}, u32[]{:S(2)}, u32[]{:S(2)}) collective-permute-start(f32[16,128]{1,0:T(8,128)S(1)} %add.124), channel_id=1, source_target_pairs={{0,12},{4,8},{8,4},{12,0},{16,28},{20,24},{24,20},{28,16},{1,13},{... | collective-permute-start | bytes 24584 | tf_op jit(solution)/shard_map/ppermute | solution.py:355
  102.0 3.7 %collective-permute-start.25 = (f32[16,128]{1,0:T(8,128)S(1)}, f32[16,128]{1,0:T(8,128)S(1)}, u32[]{:S(2)}, u32[]{:S(2)}) collective-permute-start(f32[16,128]{1,0:T(8,128)S(1)} %shard_map.55), channel_id=1, source_target_pairs={{0,2},{1,3},{2,0},{3,1},{4,6},{5,7},{6,4},{7,5},{8,10},{9,11},{10,... | collective-permute-start | bytes 24584 | tf_op jit(solution)/shard_map/ppermute | solution.py:365
  103.0 4.0 %collective-permute-start.26 = (f32[16,128]{1,0:T(8,128)S(1)}, f32[16,128]{1,0:T(8,128)S(1)}, u32[]{:S(2)}, u32[]{:S(2)}) collective-permute-start(f32[16,128]{1,0:T(8,128)S(1)} %shard_map.55), channel_id=1, source_target_pairs={{0,7},{1,6},{2,5},{3,4},{4,3},{5,2},{6,1},{7,0},{8,15},{9,14},{10,... | collective-permute-start | bytes 24584 | tf_op jit(solution)/shard_map/ppermute | solution.py:365
  104.1 3.1 %collective-permute-start.24 = (f32[16,128]{1,0:T(8,128)S(1)}, f32[16,128]{1,0:T(8,128)S(1)}, u32[]{:S(2)}, u32[]{:S(2)}) collective-permute-start(f32[16,128]{1,0:T(8,128)S(1)} %shard_map.55), channel_id=1, source_target_pairs={{0,5},{1,4},{2,7},{3,6},{4,1},{5,0},{6,3},{7,2},{8,13},{9,12},{10,... | collective-permute-start | bytes 24584 | tf_op jit(solution)/shard_map/ppermute | solution.py:365
  108.5 1.4 %collective-permute-start.27 = (f32[16,128]{1,0:T(8,128)S(1)}, f32[16,128]{1,0:T(8,128)S(1)}, u32[]{:S(2)}, u32[]{:S(2)}) collective-permute-start(f32[16,128]{1,0:T(8,128)S(1)} %shard_map.56), channel_id=1, source_target_pairs={{0,4},{4,0},{8,12},{12,8},{16,20},{20,16},{24,28},{28,24},{1,5},{5... | collective-permute-start | bytes 24584 | tf_op jit(solution)/shard_map/ppermute | solution.py:355
  109.9 4.0 %collective-permute-start.29 = (f32[16,128]{1,0:T(8,128)S(1)}, f32[16,128]{1,0:T(8,128)S(1)}, u32[]{:S(2)}, u32[]{:S(2)}) collective-permute-start(f32[16,128]{1,0:T(8,128)S(1)} %add.131), channel_id=1, source_target_pairs={{0,20},{4,16},{8,28},{12,24},{16,4},{20,0},{24,12},{28,8},{1,21},{... | collective-permute-start | bytes 24584 | tf_op jit(solution)/shard_map/ppermute | solution.py:355
  110.5 4.9 %collective-permute-start.30 = (f32[16,128]{1,0:T(8,128)S(1)}, f32[16,128]{1,0:T(8,128)S(1)}, u32[]{:S(2)}, u32[]{:S(2)}) collective-permute-start(f32[16,128]{1,0:T(8,128)S(1)} %add.131), channel_id=1, source_target_pairs={{0,28},{4,24},{8,20},{12,16},{16,12},{20,8},{24,4},{28,0},{1,29},{... | collective-permute-start | bytes 24584 | tf_op jit(solution)/shard_map/ppermute | solution.py:355
  112.2 3.2 %collective-permute-start.28 = (f32[16,128]{1,0:T(8,128)S(1)}, f32[16,128]{1,0:T(8,128)S(1)}, u32[]{:S(2)}, u32[]{:S(2)}) collective-permute-start(f32[16,128]{1,0:T(8,128)S(1)} %add.131), channel_id=1, source_target_pairs={{0,12},{4,8},{8,4},{12,0},{16,28},{20,24},{24,20},{28,16},{1,13},{... | collective-permute-start | bytes 24584 | tf_op jit(solution)/shard_map/ppermute | solution.py:355
  115.4 15.6 %copy-start = (f32[2048]{0:T(1024)S(1)}, f32[2048]{0:T(1024)}, u32[]{:S(2)}) copy-start(f32[2048]{0:T(1024)} %param.5) | copy-start | bytes 24580
  116.6 3.7 %collective-permute-start.32 = (f32[16,128]{1,0:T(8,128)S(1)}, f32[16,128]{1,0:T(8,128)S(1)}, u32[]{:S(2)}, u32[]{:S(2)}) collective-permute-start(f32[16,128]{1,0:T(8,128)S(1)} %shard_map.57), channel_id=1, source_target_pairs={{0,2},{1,3},{2,0},{3,1},{4,6},{5,7},{6,4},{7,5},{8,10},{9,11},{10,... | collective-permute-start | bytes 24584 | tf_op jit(solution)/shard_map/ppermute | solution.py:365
  118.2 4.0 %collective-permute-start.33 = (f32[16,128]{1,0:T(8,128)S(1)}, f32[16,128]{1,0:T(8,128)S(1)}, u32[]{:S(2)}, u32[]{:S(2)}) collective-permute-start(f32[16,128]{1,0:T(8,128)S(1)} %shard_map.57), channel_id=1, source_target_pairs={{0,7},{1,6},{2,5},{3,4},{4,3},{5,2},{6,1},{7,0},{8,15},{9,14},{10,... | collective-permute-start | bytes 24584 | tf_op jit(solution)/shard_map/ppermute | solution.py:365
  118.8 3.3 %collective-permute-start.31 = (f32[16,128]{1,0:T(8,128)S(1)}, f32[16,128]{1,0:T(8,128)S(1)}, u32[]{:S(2)}, u32[]{:S(2)}) collective-permute-start(f32[16,128]{1,0:T(8,128)S(1)} %shard_map.57), channel_id=1, source_target_pairs={{0,5},{1,4},{2,7},{3,6},{4,1},{5,0},{6,3},{7,2},{8,13},{9,12},{10,... | collective-permute-start | bytes 24584 | tf_op jit(solution)/shard_map/ppermute | solution.py:365
  123.5 1.2 collective-permute-start.34
  124.7 4.0 %collective-permute-start.37 = (f32[16,128]{1,0:T(8,128)S(1)}, f32[16,128]{1,0:T(8,128)S(1)}, u32[]{:S(2)}, u32[]{:S(2)}) collective-permute-start(f32[16,128]{1,0:T(8,128)S(1)} %add.138), channel_id=1, source_target_pairs={{0,20},{4,16},{8,28},{12,24},{16,4},{20,0},{24,12},{28,8},{1,21},{... | collective-permute-start | bytes 24584 | tf_op jit(solution)/shard_map/ppermute | solution.py:355
  125.9 4.9 %collective-permute-start.38 = (f32[16,128]{1,0:T(8,128)S(1)}, f32[16,128]{1,0:T(8,128)S(1)}, u32[]{:S(2)}, u32[]{:S(2)}) collective-permute-start(f32[16,128]{1,0:T(8,128)S(1)} %add.138), channel_id=1, source_target_pairs={{0,28},{4,24},{8,20},{12,16},{16,12},{20,8},{24,4},{28,0},{1,29},{... | collective-permute-start | bytes 24584 | tf_op jit(solution)/shard_map/ppermute | solution.py:355
  127.6 3.2 %collective-permute-start.36 = (f32[16,128]{1,0:T(8,128)S(1)}, f32[16,128]{1,0:T(8,128)S(1)}, u32[]{:S(2)}, u32[]{:S(2)}) collective-permute-start(f32[16,128]{1,0:T(8,128)S(1)} %add.138), channel_id=1, source_target_pairs={{0,12},{4,8},{8,4},{12,0},{16,28},{20,24},{24,20},{28,16},{1,13},{... | collective-permute-start | bytes 24584 | tf_op jit(solution)/shard_map/ppermute | solution.py:355
  127.8 3.9 %collective-permute-start.35 = (f32[16,128]{1,0:T(8,128)S(1)}, f32[16,128]{1,0:T(8,128)S(1)}, u32[]{:S(2)}, u32[]{:S(2)}) collective-permute-start(f32[16,128]{1,0:T(8,128)S(1)} %multiply_add_fusion), channel_id=1, source_target_pairs={{0,4},{4,0},{8,12},{12,8},{16,20},{20,16},{24,28},{28,24},{1,5},{5... | collective-permute-start | bytes 24584 | tf_op jit(solution)/shard_map/ppermute | solution.py:355

commit v3 on v2

--- a/solution.py
+++ b/solution.py
@@ -15,6 +15,7 @@
 SUB = 8
 MIB = 1024 * 1024
 TILE = 256
+DEEP = 512
 HEAD = 40.0
 ROW_LOW, ROW_HIGH = 2.0**20, 2.0**80
 SCALE_LOW, COLUMN_LOW = 2.0**-60, 2.0**-30
@@ -119,8 +120,8 @@
             cols = pl.ds(pl.multiple_of(start + t * width, LANES), width)
             out = pl.ds(pl.multiple_of(place + t * width, LANES), width)
             total = None
-            for c in range(left.shape[0] // TILE):
-                rows = slice(c * TILE, (c + 1) * TILE)
+            for c in range(left.shape[0] // DEEP):
+                rows = slice(c * DEEP, (c + 1) * DEEP)
                 tile = jnp.exp2(jnp.dot(left[rows, :], right[:, cols], preferred_element_type=jnp.float32))
                 ratios[rows, out] = tile
                 part = fold_rows(jnp.add, tile)
@@ -139,24 +140,28 @@
         points[:, pl.ds(start, width)] = piece[...]
 
 
-def own_scores_kernel(place, own_src, own_tgt, own_g0, *refs):
-    lse, norms, left, right, base, flag, ratios, stack, points, acc, held_src, held_tgt, g0, sems = refs[-14:]
-    tgt = refs[:-14]
+def own_pieces_kernel(own_src, own_tgt, own_g0, norms, right, tgt, g0, held_src, sems):
     copies = [
         pltpu.make_async_copy(source, target, sems.at[k])
-        for k, (source, target) in enumerate(((own_src, held_src), (own_tgt, held_tgt), (own_g0, g0)))
+        for k, (source, target) in enumerate(((own_src, held_src), (own_tgt, tgt), (own_g0, g0)))
     ]
     for copy in copies:
         copy.start()
     for copy in copies:
         copy.wait()
-    depth, width = held_src.shape
-    first = 6 * depth
     x = held_src[...]
     store_rows(norms, jnp.sum(x * x, axis=0, keepdims=True))
-    place_sources(x, right, slice(0, width))
-
-    place_pieces(points, place[1], (held_tgt, *tgt))
+    place_sources(x, right, slice(0, x.shape[1]))
+
+
+def own_scores_kernel(place, own_right, g0, *refs):
+    lse, left, right, base, flag, ratios, stack, points, acc = refs[-9:]
+    tgt = refs[:-9]
+    depth = tgt[0].shape[0]
+    first = 6 * depth
+    width = right.shape[1]
+
+    place_pieces(points, place[1], tgt)
     ntgt = left.shape[0]
     y = points[...]
     gamma = ALPHA * (g0[...] - jnp.sum(y * y, axis=0, keepdims=True))
@@ -174,7 +179,8 @@
     for c in range(ntgt // TILE):
         left[c * TILE : (c + 1) * TILE, :] = stack[:, c * TILE : (c + 1) * TILE].T
 
-    fine = guarded_sums(left, right, [(0, place[0] * width, width, 0)], base[:, :1], lse, ratios)
+    fine = guarded_sums(left, own_right, [(0, place[0] * width, width, 0)], base[:, :1], lse, ratios)
+    right[...] = own_right[...]
     flag[...] = jnp.full(flag.shape, jnp.where(fine, 1.0, 0.0), jnp.float32)
 
     @pl.when(jnp.logical_not(fine))
@@ -355,18 +361,30 @@
     return lax.ppermute(value, axis, [(k, k ^ distance) for k in range(lax.axis_size(axis))])
 
 
+def parity(value):
+    return sum((value >> k) & 1 for k in range(lax.axis_size("cols").bit_length())) % 2
+
+
 def same_block(value, distance):
     nrows, ncols = lax.axis_size("rows"), lax.axis_size("cols")
     perm = [
-        (row * ncols + col, (row ^ (distance & 1)) * ncols + (col ^ distance))
+        (row * ncols + col, (row ^ parity(distance)) * ncols + (col ^ distance))
         for row in range(nrows)
         for col in range(ncols)
     ]
     return lax.ppermute(value, ("rows", "cols"), perm)
 
 
+def fold_ends(reduce, values):
+    first = lax.optimization_barrier(reduce([values[0], values[-1]]))
+    values = [first] + [reduce([values[-1 - k], values[k]]) for k in range(1, len(values) // 2)]
+    while len(values) > 1:
+        values = [reduce([values[k], values[-1 - k]]) for k in range(len(values) // 2)]
+    return values[0]
+
+
 def combine_cols(reduce, value):
-    return reduce([value] + [same_block(value, d) for d in range(1, lax.axis_size("cols"))])
+    return fold_ends(reduce, [value] + [same_block(value, d) for d in range(1, lax.axis_size("cols"))])
 
 
 def add_cores(reduce, value):
@@ -374,7 +392,7 @@
 
 
 def combine_chips(reduce, value):
-    return reduce([value] + [swap(value, "rows", d) for d in range(3, lax.axis_size("rows"), 2)])
+    return fold_ends(reduce, [value] + [swap(value, "rows", d) for d in range(3, lax.axis_size("rows"), 2)])
 
 
 def combine_rows(reduce, value):
@@ -386,13 +404,14 @@
 
 
 def gather_rows(value):
-    far = {0: value}
-    for d in range(3, lax.axis_size("rows"), 2):
-        far[d] = swap(value, "rows", d)
-    pieces = dict(far)
-    for d, piece in far.items():
-        pieces[d ^ 1] = swap(piece, "rows", 1)
-    return [pieces[d] for d in range(1, lax.axis_size("rows"))]
+    count = lax.axis_size("rows")
+    pieces = {1: swap(value, "rows", 1)}
+    for d in range(3, count, 2):
+        pieces[d] = swap(value, "rows", d)
+    pieces[3], pieces[1] = lax.optimization_barrier((pieces[3], pieces[1]))
+    for d in range(3, count, 2):
+        pieces[d ^ 1] = swap(pieces[d], "rows", 1)
+    return [pieces[d] for d in range(1, count)]
 
 
 def call(kernel, out_shape, nin, scratch=(), limit=8, aliases=None, smem=0, hbm=0):
@@ -436,10 +455,26 @@
     piece = source_points.shape[1]
     by_piece = jax.ShapeDtypeStruct((piece // LANES, LANES), f32)
     line = jax.ShapeDtypeStruct((1, LANES), f32)
-    own_lse, own_norms, left, own_right, base, own_flag, ratios = call(
+    own_norms, own_right, own_tgt, own_g0 = call(
+        own_pieces_kernel,
+        [
+            by_piece,
+            pltpu.VMEM((stack, piece), bf16),
+            jax.ShapeDtypeStruct(target_points.shape, f32),
+            jax.ShapeDtypeStruct((1, tgt_count), f32),
+        ],
+        3,
+        [pltpu.VMEM(source_points.shape, f32), pltpu.SemaphoreType.DMA((3,))],
+        hbm=3,
+    )(
+        *(
+            pltpu.with_memory_space_constraint(own, pltpu.HBM)
+            for own in (source_points, target_points, target_init.reshape(1, tgt_count))
+        ),
+    )
+    own_lse, left, own_right, base, own_flag, ratios = call(
         own_scores_kernel,
         [
-            by_piece,
             by_piece,
             pltpu.VMEM((tgt_count, stack), bf16),
             pltpu.VMEM((stack, piece), bf16),
@@ -452,22 +487,10 @@
             pltpu.VMEM((stack, tgt_count), bf16),
             pltpu.VMEM((depth, tgt_count), f32),
             pltpu.VMEM((SUB, piece), f32),
-            pltpu.VMEM(source_points.shape, f32),
-            pltpu.VMEM(target_points.shape, f32),
-            pltpu.VMEM((1, tgt_count), f32),
-            pltpu.SemaphoreType.DMA((3,)),
         ],
         limit=16,
         smem=1,
-        hbm=3,
-    )(
-        place,
-        *(
-            pltpu.with_memory_space_constraint(own, pltpu.HBM)
-            for own in (source_points, target_points, target_init.reshape(1, tgt_count))
-        ),
-        *targets,
-    )
+    )(place, pin(own_right), own_g0, own_tgt, *targets)
     left = pin(left)
     lse, norms, right, flag, ratios = call(
         scores_kernel,
@@ -492,26 +515,28 @@
         4,
     )(ratios, scale, peaks, combine_rows(lse2, lse))
     for step in range(1, ITERS):
+        last = step == ITERS - 1
         row_total = combine_cols(add_all, total)
+        if last:
+            f = (phi + (log_ntgt - jnp.log2(row_total))) * (1.0 / ALPHA) + norms
+            other_f = swap(f, "rows", 1)
         (total,) = call(
             functools.partial(columns_kernel, float(ntgt)),
             [by_tgt],
             4,
             [row_src],
         )(ratios, scale, weights, row_total)
-        total = add_cores(add_all, total)
-        if step == ITERS - 1:
-            total, row_total = lax.optimization_barrier((total, row_total))
-        total = combine_chips(add_all, total)
-        if step < ITERS - 1:
+        if last:
+            total, f, other_f = lax.optimization_barrier((total, f, other_f))
+        total = combine_rows(add_all, total)
+        if not last:
             (total,) = call(
                 functools.partial(rows_kernel, float(nsrc)),
                 [by_src],
                 4,
             )(ratios, scale, weights, total)
-    f = (phi + (log_ntgt - jnp.log2(row_total))) * (1.0 / ALPHA) + norms
     column = lax.broadcasted_iota(jnp.int32, f.shape, 0) // (piece // LANES)
-    f = jnp.where((column - lax.axis_index("cols")) % 2 == 0, f, swap(f, "rows", 1))
+    f = jnp.where(parity(column ^ lax.axis_index("cols")) == 0, f, other_f)
     (delta,) = call(functools.partial(finish_kernel, log_nsrc), [by_tgt], 2)(shift, total)
     delta = delta.reshape(-1, SUB, LANES).transpose(0, 2, 1).reshape(-1)
     return f.reshape(-1), target_init + delta

time: 133 us -> 130 us (0.977)
  waiting for transfers between devices: 24 us -> 17.7 us
  starting transfers between devices: 39.5 us -> 43.3 us
    ppermute x24, waiting for transfers between devices: 14.7 us -> 10 us  [swap(): lax.ppermute(value, axis, [(k, k ^ distance) for k in range(lax.axis_size...]
    ppermute x24, starting transfers between devices: 21.9 us -> 25.1 us  [swap(): lax.ppermute(value, axis, [(k, k ^ distance) for k in range(lax.axis_size...]
    ppermute x15, waiting for transfers between devices: 9.25 us -> 7.67 us  [same_block(): return lax.ppermute(value, ('rows', 'cols'), perm)]
    pallas_call x1 -> x2, Pallas kernels: 8.94 us -> 8.97 us  [the longest x1 8.07 us: body(): call(own_scores_kernel, [by_piece, pltpu.VMEM((tgt_count, stack), bf16),...]
  transfers between devices with their start and end apart: 39 -> 39, of which waited for: 24 -> 22; matrix products, arithmetic and copies ran while one was open for 1% -> 1% of each run, Pallas kernels for 7% -> 8%
where the time goes in v3:
time: 130 us
  Pallas kernels  66.4 us (51%)
  starting transfers between devices  43.3 us (33%)
  waiting for transfers between devices  17.7 us (14%)
  other arithmetic  1.55 us (1%)
    pallas_call x1, Pallas kernels, body(): call(scores_kernel, [by_src, by_src, pltpu.VMEM((stack, src_count), bf16)...  28.9 us
    ppermute x24, starting transfers between devices, swap(): lax.ppermute(value, axis, [(k, k ^ distance) for k in range(lax.axis_size...  25.1 us
    pallas_call x1, Pallas kernels, body(): call(functools.partial(first_columns_kernel, log_ntgt, 6 * depth), [squar...  20.9 us
    ppermute x15, starting transfers between devices, same_block(): return lax.ppermute(value, ('rows', 'cols'), perm)  18.1 us
    ppermute x24, waiting for transfers between devices, swap(): lax.ppermute(value, axis, [(k, k ^ distance) for k in range(lax.axis_size...  10 us
    pallas_call x1, Pallas kernels, body(): call(own_scores_kernel, [by_piece, pltpu.VMEM((tgt_count, stack), bf16),...  8.07 us
    ppermute x15, waiting for transfers between devices, same_block(): return lax.ppermute(value, ('rows', 'cols'), perm)  7.67 us
    pallas_call x3, Pallas kernels, body(): call(functools.partial(columns_kernel, float(ntgt)), [by_tgt], 4, [row_src])  3.98 us
  transfers between devices with their start and end apart: 39, of which 22 were waited for; matrix products, arithmetic and copies ran while one was open for 1% of the time, Pallas kernels for 8%

profile of v3, /device:TPU:0, one launch (start us, length us, event | category | flops | bytes accessed | tf_op | source)
XLA Modules:
  0.0 129.9 jit_solution(1177807722216846523)
XLA Ops:
  0.6 2.5 %collective-permute-start = (f32[32,256]{1,0:T(8,128)}, f32[32,256]{1,0:T(8,128)S(1)}, u32[]{:S(2)}, u32[]{:S(2)}) collective-permute-start(f32[32,256]{1,0:T(8,128)} %own_tgt.1), channel_id=1, source_target_pairs={{0,12},{4,8},{8,4},{12,0},{16,28},{20,24},{24,20},{28,16},{1,13},{... | collective-permute-start | bytes 98312 | tf_op jit(solution)/shard_map/ppermute | solution.py:361
  3.8 2.2 %collective-permute-start.3 = (f32[32,256]{1,0:T(8,128)}, f32[32,256]{1,0:T(8,128)S(1)}, u32[]{:S(2)}, u32[]{:S(2)}) collective-permute-start(f32[32,256]{1,0:T(8,128)} %own_tgt.1), channel_id=1, source_target_pairs={{0,20},{4,16},{8,28},{12,24},{16,4},{20,0},{24,12},{28,8},{1,21},{... | collective-permute-start | bytes 98312 | tf_op jit(solution)/shard_map/ppermute | solution.py:361
  6.6 1.4 %collective-permute-start.7 = (f32[32,512]{1,0:T(8,128)}, f32[32,512]{1,0:T(8,128)S(1)}, u32[]{:S(2)}, u32[]{:S(2)}) collective-permute-start(f32[32,512]{1,0:T(8,128)} %own_src.1), channel_id=1, source_target_pairs={{0,5},{1,4},{2,7},{3,6},{4,1},{5,0},{6,3},{7,2},{8,13},{9,12},{10,... | collective-permute-start | bytes 196616 | tf_op jit(solution)/shard_map/ppermute | solution.py:375
  8.0 1.4 %collective-permute-start.8 = (f32[32,512]{1,0:T(8,128)}, f32[32,512]{1,0:T(8,128)S(1)}, u32[]{:S(2)}, u32[]{:S(2)}) collective-permute-start(f32[32,512]{1,0:T(8,128)} %own_src.1), channel_id=1, source_target_pairs={{0,6},{1,7},{2,4},{3,5},{4,2},{5,3},{6,0},{7,1},{8,14},{9,15},{10,... | collective-permute-start | bytes 196616 | tf_op jit(solution)/shard_map/ppermute | solution.py:375
  9.4 2.3 %collective-permute-start.9 = (f32[32,512]{1,0:T(8,128)}, f32[32,512]{1,0:T(8,128)S(1)}, u32[]{:S(2)}, u32[]{:S(2)}) collective-permute-start(f32[32,512]{1,0:T(8,128)} %own_src.1), channel_id=1, source_target_pairs={{0,3},{1,2},{2,1},{3,0},{4,7},{5,6},{6,5},{7,4},{8,11},{9,10},{10,... | collective-permute-start | bytes 196616 | tf_op jit(solution)/shard_map/ppermute | solution.py:375
  12.3 0.9 shard_map.50
  13.2 8.1 %shard_map.51 = (f32[4,128]{1,0:T(4,128)S(1)}, bf16[2048,256]{1,0:T(8,128)(2,1)S(1)}, bf16[256,512]{1,0:T(8,128)(2,1)S(1)}, f32[1,128]{1,0:T(1,128)S(1)}, f32[1,...) custom-call(s32[2]{0:T(128)S(1)} %pad_add_fusion.place, bf16[256,512]{1,0:T(8,128)(2,1)S(1)} %get-tuple-element.30.own_right, ...), custom_call_target="tpu_custom_call" | custom-call | tf_op jit(solution)/shard_map/pallas_call | solution.py:475
  21.3 28.9 %shard_map.52 = (f32[16,128]{1,0:T(8,128)S(1)}, f32[16,128]{1,0:T(8,128)S(1)}, bf16[256,2048]{1,0:T(8,128)(2,1)S(1)}, f32[1,128]{1,0:T(1,128)S(1)}, f32[2048,2048]{1,0:T(8,128)S(1)}) custom-call(s32[2]{0:T(128)S(1)} %pad_add_fusion.place, bf16[2048,256]{1,0:T(8,128)(2,1)S(1)} %get-tuple-element.35.left, ...), custom_call_target="tpu_custom_call", output_to_operand_aliasing={{4}: (7, {})} | custom-call | tf_op jit(solution)/shard_map/pallas_call | solution.py:495
  50.2 2.4 %collective-permute-start.10 = (f32[16,128]{1,0:T(8,128)S(1)}, f32[16,128]{1,0:T(8,128)S(1)}, u32[]{:S(2)}, u32[]{:S(2)}) collective-permute-start(f32[16,128]{1,0:T(8,128)S(1)} %get-tuple-element.43), channel_id=1, source_target_pairs={{0,3},{1,2},{2,1},{3,0},{4,7},{5,6},{6,5},{7,4},{8,11},{9,10},{10,... | collective-permute-start | bytes 24584 | tf_op jit(solution)/shard_map/ppermute | solution.py:375
  53.4 1.3 %collective-permute-done.10 = f32[16,128]{1,0:T(8,128)S(1)} collective-permute-done((f32[16,128]{1,0:T(8,128)S(1)}, f32[16,128]{1,0:T(8,128)S(1)}, u32[]{:S(2)}, u32[]{:S(2)}) %collective-permute-start.10) | collective-permute-done | bytes 8224 | tf_op jit(solution)/shard_map/ppermute | solution.py:375
  54.8 0.9 collective-permute-done.11
  55.9 20.9 %shard_map.53 = (f32[2048,2048]{1,0:T(8,128)S(1)}, bf16[256,2048]{1,0:T(8,128)(2,1)S(1)}, f32[16,128]{1,0:T(8,128)S(1)}, f32[16,128]{1,0:T(8,128)S(1)}, f32[16,128]{1,0:T(8,128)S(1)}, /*index=5*/f32[16,128]{1,0:T(8,128)S(1)}) custom-call(bf16[2048,256]{1,0:T(8,128)(2,1)S(1)} %get-tuple-element.35.left, ...), custom_call_target="tpu_custom_call", output_to_operand_aliasing={{0}: (4, {}), {1}: (5, {})} | custom-call | tf_op jit(solution)/shard_map/pallas_call | solution.py:504
  77.3 0.8 collective-permute-done.13
  78.1 1.7 %collective-permute-start.14 = (f32[16,128]{1,0:T(8,128)S(1)}, f32[16,128]{1,0:T(8,128)S(1)}, u32[]{:S(2)}, u32[]{:S(2)}) collective-permute-start(f32[16,128]{1,0:T(8,128)S(1)} %multiply_add_fusion.3), channel_id=1, source_target_pairs={{0,28},{4,24},{8,20},{12,16},{16,12},{20,8},{24,4},{28,0},{1,29},{... | collective-permute-start | bytes 24584 | tf_op jit(solution)/shard_map/ppermute | solution.py:361
  79.8 2.4 %collective-permute-start.16 = (f32[16,128]{1,0:T(8,128)S(1)}, f32[16,128]{1,0:T(8,128)S(1)}, u32[]{:S(2)}, u32[]{:S(2)}) collective-permute-start(f32[16,128]{1,0:T(8,128)S(1)} %multiply_add_fusion.3), channel_id=1, source_target_pairs={{0,12},{4,8},{8,4},{12,0},{16,28},{20,24},{24,20},{28,16},{1,13},{... | collective-permute-start | bytes 24584 | tf_op jit(solution)/shard_map/ppermute | solution.py:361
  82.2 0.8 collective-permute-done.14
  83.1 0.7 collective-permute-done.15
  83.8 1.2 shard_map.54
  85.0 1.6 %collective-permute-start.17 = (f32[16,128]{1,0:T(8,128)S(1)}, f32[16,128]{1,0:T(8,128)S(1)}, u32[]{:S(2)}, u32[]{:S(2)}) collective-permute-start(f32[16,128]{1,0:T(8,128)S(1)} %get-tuple-element.51), channel_id=1, source_target_pairs={{0,3},{1,2},{2,1},{3,0},{4,7},{5,6},{6,5},{7,4},{8,11},{9,10},{10,... | collective-permute-start | bytes 24584 | tf_op jit(solution)/shard_map/ppermute | solution.py:375
  86.8 1.6 %collective-permute-start.19 = (f32[16,128]{1,0:T(8,128)S(1)}, f32[16,128]{1,0:T(8,128)S(1)}, u32[]{:S(2)}, u32[]{:S(2)}) collective-permute-start(f32[16,128]{1,0:T(8,128)S(1)} %get-tuple-element.51), channel_id=1, source_target_pairs={{0,5},{1,4},{2,7},{3,6},{4,1},{5,0},{6,3},{7,2},{8,13},{9,12},{10,... | collective-permute-start | bytes 24584 | tf_op jit(solution)/shard_map/ppermute | solution.py:375
  88.3 1.3 %collective-permute-done.17 = f32[16,128]{1,0:T(8,128)S(1)} collective-permute-done((f32[16,128]{1,0:T(8,128)S(1)}, f32[16,128]{1,0:T(8,128)S(1)}, u32[]{:S(2)}, u32[]{:S(2)}) %collective-permute-start.17) | collective-permute-done | bytes 8224 | tf_op jit(solution)/shard_map/ppermute | solution.py:375
  89.8 1.3 %shard_map.55 = f32[16,128]{1,0:T(8,128)S(1)} custom-call(f32[2048,2048]{1,0:T(8,128)S(1)} %get-tuple-element.46.ratios, f32[16,128]{1,0:T(8,128)S(1)} %get-tuple-element.47.scale, f32[16,128]{1,0:T(8,128)S(1)} %get-tuple-element.50.weights, f32[16,128]{1,0:T(8,128)S(1)} %add_add_fusion.5.total), custom_call_target="tpu_custom_call" | custom-call | tf_op jit(solution)/shard_map/pallas_call | solution.py:523
  91.8 0.8 collective-permute-done.20
  92.7 2.1 %collective-permute-start.21 = (f32[16,128]{1,0:T(8,128)S(1)}, f32[16,128]{1,0:T(8,128)S(1)}, u32[]{:S(2)}, u32[]{:S(2)}) collective-permute-start(f32[16,128]{1,0:T(8,128)S(1)} %add.148), channel_id=1, source_target_pairs={{0,28},{4,24},{8,20},{12,16},{16,12},{20,8},{24,4},{28,0},{1,29},{... | collective-permute-start | bytes 24584 | tf_op jit(solution)/shard_map/ppermute | solution.py:361
  95.4 1.4 %collective-permute-start.23 = (f32[16,128]{1,0:T(8,128)S(1)}, f32[16,128]{1,0:T(8,128)S(1)}, u32[]{:S(2)}, u32[]{:S(2)}) collective-permute-start(f32[16,128]{1,0:T(8,128)S(1)} %add.148), channel_id=1, source_target_pairs={{0,12},{4,8},{8,4},{12,0},{16,28},{20,24},{24,20},{28,16},{1,13},{... | collective-permute-start | bytes 24584 | tf_op jit(solution)/shard_map/ppermute | solution.py:361
  96.7 0.8 collective-permute-done.21
  97.5 1.2 collective-permute-done.22
  98.7 1.2 shard_map.56
  99.9 2.4 %collective-permute-start.24 = (f32[16,128]{1,0:T(8,128)S(1)}, f32[16,128]{1,0:T(8,128)S(1)}, u32[]{:S(2)}, u32[]{:S(2)}) collective-permute-start(f32[16,128]{1,0:T(8,128)S(1)} %shard_map.56), channel_id=1, source_target_pairs={{0,3},{1,2},{2,1},{3,0},{4,7},{5,6},{6,5},{7,4},{8,11},{9,10},{10,... | collective-permute-start | bytes 24584 | tf_op jit(solution)/shard_map/ppermute | solution.py:375
  102.3 0.9 collective-permute-start.26
  103.2 1.3 %collective-permute-done.24 = f32[16,128]{1,0:T(8,128)S(1)} collective-permute-done((f32[16,128]{1,0:T(8,128)S(1)}, f32[16,128]{1,0:T(8,128)S(1)}, u32[]{:S(2)}, u32[]{:S(2)}) %collective-permute-start.24) | collective-permute-done | bytes 8224 | tf_op jit(solution)/shard_map/ppermute | solution.py:375
  104.6 0.9 collective-permute-done.25
  105.4 1.3 %shard_map.57 = f32[16,128]{1,0:T(8,128)S(1)} custom-call(f32[2048,2048]{1,0:T(8,128)S(1)} %get-tuple-element.46.ratios, f32[16,128]{1,0:T(8,128)S(1)} %get-tuple-element.47.scale, f32[16,128]{1,0:T(8,128)S(1)} %get-tuple-element.50.weights, f32[16,128]{1,0:T(8,128)S(1)} %add_add_fusion.3.total), custom_call_target="tpu_custom_call" | custom-call | tf_op jit(solution)/shard_map/pallas_call | solution.py:523
  107.4 0.8 collective-permute-done.27
  108.2 1.6 %collective-permute-start.28 = (f32[16,128]{1,0:T(8,128)S(1)}, f32[16,128]{1,0:T(8,128)S(1)}, u32[]{:S(2)}, u32[]{:S(2)}) collective-permute-start(f32[16,128]{1,0:T(8,128)S(1)} %add.155), channel_id=1, source_target_pairs={{0,28},{4,24},{8,20},{12,16},{16,12},{20,8},{24,4},{28,0},{1,29},{... | collective-permute-start | bytes 24584 | tf_op jit(solution)/shard_map/ppermute | solution.py:361
  110.5 1.8 %collective-permute-start.30 = (f32[16,128]{1,0:T(8,128)S(1)}, f32[16,128]{1,0:T(8,128)S(1)}, u32[]{:S(2)}, u32[]{:S(2)}) collective-permute-start(f32[16,128]{1,0:T(8,128)S(1)} %add.155), channel_id=1, source_target_pairs={{0,12},{4,8},{8,4},{12,0},{16,28},{20,24},{24,20},{28,16},{1,13},{... | collective-permute-start | bytes 24584 | tf_op jit(solution)/shard_map/ppermute | solution.py:361
  112.3 0.8 collective-permute-done.28
  113.1 0.7 collective-permute-done.29
  113.8 1.2 shard_map.58
  115.0 1.6 %collective-permute-start.31 = (f32[16,128]{1,0:T(8,128)S(1)}, f32[16,128]{1,0:T(8,128)S(1)}, u32[]{:S(2)}, u32[]{:S(2)}) collective-permute-start(f32[16,128]{1,0:T(8,128)S(1)} %shard_map.58), channel_id=1, source_target_pairs={{0,3},{1,2},{2,1},{3,0},{4,7},{5,6},{6,5},{7,4},{8,11},{9,10},{10,... | collective-permute-start | bytes 24584 | tf_op jit(solution)/shard_map/ppermute | solution.py:375
  116.8 1.5 %collective-permute-start.33 = (f32[16,128]{1,0:T(8,128)S(1)}, f32[16,128]{1,0:T(8,128)S(1)}, u32[]{:S(2)}, u32[]{:S(2)}) collective-permute-start(f32[16,128]{1,0:T(8,128)S(1)} %shard_map.58), channel_id=1, source_target_pairs={{0,5},{1,4},{2,7},{3,6},{4,1},{5,0},{6,3},{7,2},{8,13},{9,12},{10,... | collective-permute-start | bytes 24584 | tf_op jit(solution)/shard_map/ppermute | solution.py:375
  118.3 1.3 %collective-permute-done.31 = f32[16,128]{1,0:T(8,128)S(1)} collective-permute-done((f32[16,128]{1,0:T(8,128)S(1)}, f32[16,128]{1,0:T(8,128)S(1)}, u32[]{:S(2)}, u32[]{:S(2)}) %collective-permute-start.31) | collective-permute-done | bytes 8224 | tf_op jit(solution)/shard_map/ppermute | solution.py:375
  120.6 1.3 %shard_map.59 = f32[16,128]{1,0:T(8,128)S(1)} custom-call(f32[2048,2048]{1,0:T(8,128)S(1)} %get-tuple-element.46.ratios, f32[16,128]{1,0:T(8,128)S(1)} %get-tuple-element.47.scale, f32[16,128]{1,0:T(8,128)S(1)} %get-tuple-element.50.weights, f32[16,128]{1,0:T(8,128)S(1)} %get-tuple-element.59.total), custom_call_target="tpu_custom_call" | custom-call | tf_op jit(solution)/shard_map/pallas_call | solution.py:523
  122.0 1.1 collective-permute-done.35
  123.1 1.9 %collective-permute-start.36 = (f32[16,128]{1,0:T(8,128)S(1)}, f32[16,128]{1,0:T(8,128)S(1)}, u32[]{:S(2)}, u32[]{:S(2)}) collective-permute-start(f32[16,128]{1,0:T(8,128)S(1)} %add.164), channel_id=1, source_target_pairs={{0,28},{4,24},{8,20},{12,16},{16,12},{20,8},{24,4},{28,0},{1,29},{... | collective-permute-start | bytes 24584 | tf_op jit(solution)/shard_map/ppermute | solution.py:361
  125.0 0.8 collective-permute-start.37
  125.8 1.2 collective-permute-start.38
  128.0 1.0 collective-permute-done.37
  (70 shorter events, 9.5 us)
Async XLA Ops:
  0.6 5.4 %collective-permute-start = (f32[32,256]{1,0:T(8,128)}, f32[32,256]{1,0:T(8,128)S(1)}, u32[]{:S(2)}, u32[]{:S(2)}) collective-permute-start(f32[32,256]{1,0:T(8,128)} %own_tgt.1), channel_id=1, source_target_pairs={{0,12},{4,8},{8,4},{12,0},{16,28},{20,24},{24,20},{28,16},{1,13},{... | collective-permute-start | bytes 98312 | tf_op jit(solution)/shard_map/ppermute | solution.py:361
  3.2 2.9 %collective-permute-start.1 = (f32[32,256]{1,0:T(8,128)}, f32[32,256]{1,0:T(8,128)S(1)}, u32[]{:S(2)}, u32[]{:S(2)}) collective-permute-start(f32[32,256]{1,0:T(8,128)} %own_tgt.1), channel_id=1, source_target_pairs={{0,4},{4,0},{8,12},{12,8},{16,20},{20,16},{24,28},{28,24},{1,5},{5... | collective-permute-start | bytes 98312 | tf_op jit(solution)/shard_map/ppermute | solution.py:361
  3.8 5.5 %collective-permute-start.3 = (f32[32,256]{1,0:T(8,128)}, f32[32,256]{1,0:T(8,128)S(1)}, u32[]{:S(2)}, u32[]{:S(2)}) collective-permute-start(f32[32,256]{1,0:T(8,128)} %own_tgt.1), channel_id=1, source_target_pairs={{0,20},{4,16},{8,28},{12,24},{16,4},{20,0},{24,12},{28,8},{1,21},{... | collective-permute-start | bytes 98312 | tf_op jit(solution)/shard_map/ppermute | solution.py:361
  6.0 5.6 %collective-permute-start.5 = (f32[32,256]{1,0:T(8,128)}, f32[32,256]{1,0:T(8,128)S(1)}, u32[]{:S(2)}, u32[]{:S(2)}) collective-permute-start(f32[32,256]{1,0:T(8,128)} %own_tgt.1), channel_id=1, source_target_pairs={{0,28},{4,24},{8,20},{12,16},{16,12},{20,8},{24,4},{28,0},{1,29},{... | collective-permute-start | bytes 98312 | tf_op jit(solution)/shard_map/ppermute | solution.py:361
  6.0 5.8 %collective-permute-start.2 = (f32[32,256]{1,0:T(8,128)S(1)}, f32[32,256]{1,0:T(8,128)S(1)}, u32[]{:S(2)}, u32[]{:S(2)}) collective-permute-start(f32[32,256]{1,0:T(8,128)S(1)} %collective-permute-done.refs_3_), channel_id=1, source_target_pairs={{0,4},{4,0},{8,12},{12,8},{16,20},{20,16},{24,28},{28,24},{1,5},{5... | collective-permute-start | bytes 98312 | tf_op jit(solution)/shard_map/ppermute | solution.py:361
  6.6 14.6 %collective-permute-start.7 = (f32[32,512]{1,0:T(8,128)}, f32[32,512]{1,0:T(8,128)S(1)}, u32[]{:S(2)}, u32[]{:S(2)}) collective-permute-start(f32[32,512]{1,0:T(8,128)} %own_src.1), channel_id=1, source_target_pairs={{0,5},{1,4},{2,7},{3,6},{4,1},{5,0},{6,3},{7,2},{8,13},{9,12},{10,... | collective-permute-start | bytes 196616 | tf_op jit(solution)/shard_map/ppermute | solution.py:375
  8.0 13.3 %collective-permute-start.8 = (f32[32,512]{1,0:T(8,128)}, f32[32,512]{1,0:T(8,128)S(1)}, u32[]{:S(2)}, u32[]{:S(2)}) collective-permute-start(f32[32,512]{1,0:T(8,128)} %own_src.1), channel_id=1, source_target_pairs={{0,6},{1,7},{2,4},{3,5},{4,2},{5,3},{6,0},{7,1},{8,14},{9,15},{10,... | collective-permute-start | bytes 196616 | tf_op jit(solution)/shard_map/ppermute | solution.py:375
  9.4 11.9 %collective-permute-start.9 = (f32[32,512]{1,0:T(8,128)}, f32[32,512]{1,0:T(8,128)S(1)}, u32[]{:S(2)}, u32[]{:S(2)}) collective-permute-start(f32[32,512]{1,0:T(8,128)} %own_src.1), channel_id=1, source_target_pairs={{0,3},{1,2},{2,1},{3,0},{4,7},{5,6},{6,5},{7,4},{8,11},{9,10},{10,... | collective-permute-start | bytes 196616 | tf_op jit(solution)/shard_map/ppermute | solution.py:375
  11.7 1.5 %collective-permute-start.4 = (f32[32,256]{1,0:T(8,128)S(1)}, f32[32,256]{1,0:T(8,128)S(1)}, u32[]{:S(2)}, u32[]{:S(2)}) collective-permute-start(f32[32,256]{1,0:T(8,128)S(1)} %collective-permute-done.3.refs_5_), channel_id=1, source_target_pairs={{0,4},{4,0},{8,12},{12,8},{16,20},{20,16},{24,28},{28,24},{1,5},{5... | collective-permute-start | bytes 98312 | tf_op jit(solution)/shard_map/ppermute | solution.py:361
  11.9 1.3 collective-permute-start.6
  50.2 4.6 %collective-permute-start.10 = (f32[16,128]{1,0:T(8,128)S(1)}, f32[16,128]{1,0:T(8,128)S(1)}, u32[]{:S(2)}, u32[]{:S(2)}) collective-permute-start(f32[16,128]{1,0:T(8,128)S(1)} %get-tuple-element.43), channel_id=1, source_target_pairs={{0,3},{1,2},{2,1},{3,0},{4,7},{5,6},{6,5},{7,4},{8,11},{9,10},{10,... | collective-permute-start | bytes 24584 | tf_op jit(solution)/shard_map/ppermute | solution.py:375
  52.6 3.1 %collective-permute-start.11 = (f32[16,128]{1,0:T(8,128)S(1)}, f32[16,128]{1,0:T(8,128)S(1)}, u32[]{:S(2)}, u32[]{:S(2)}) collective-permute-start(f32[16,128]{1,0:T(8,128)S(1)} %get-tuple-element.43), channel_id=1, source_target_pairs={{0,6},{1,7},{2,4},{3,5},{4,2},{5,3},{6,0},{7,1},{8,14},{9,15},{10,... | collective-permute-start | bytes 24584 | tf_op jit(solution)/shard_map/ppermute | solution.py:375
  52.8 3.1 %collective-permute-start.12 = (f32[16,128]{1,0:T(8,128)S(1)}, f32[16,128]{1,0:T(8,128)S(1)}, u32[]{:S(2)}, u32[]{:S(2)}) collective-permute-start(f32[16,128]{1,0:T(8,128)S(1)} %get-tuple-element.43), channel_id=1, source_target_pairs={{0,5},{1,4},{2,7},{3,6},{4,1},{5,0},{6,3},{7,2},{8,13},{9,12},{10,... | collective-permute-start | bytes 24584 | tf_op jit(solution)/shard_map/ppermute | solution.py:375
  76.7 1.3 %collective-permute-start.13 = (f32[16,128]{1,0:T(8,128)S(1)}, f32[16,128]{1,0:T(8,128)S(1)}, u32[]{:S(2)}, u32[]{:S(2)}) collective-permute-start(f32[16,128]{1,0:T(8,128)S(1)} %get-tuple-element.49), channel_id=1, source_target_pairs={{0,4},{4,0},{8,12},{12,8},{16,20},{20,16},{24,28},{28,24},{1,5},{5... | collective-permute-start | bytes 24584 | tf_op jit(solution)/shard_map/ppermute | solution.py:361
  78.1 4.9 %collective-permute-start.14 = (f32[16,128]{1,0:T(8,128)S(1)}, f32[16,128]{1,0:T(8,128)S(1)}, u32[]{:S(2)}, u32[]{:S(2)}) collective-permute-start(f32[16,128]{1,0:T(8,128)S(1)} %multiply_add_fusion.3), channel_id=1, source_target_pairs={{0,28},{4,24},{8,20},{12,16},{16,12},{20,8},{24,4},{28,0},{1,29},{... | collective-permute-start | bytes 24584 | tf_op jit(solution)/shard_map/ppermute | solution.py:361
  79.8 4.0 %collective-permute-start.15 = (f32[16,128]{1,0:T(8,128)S(1)}, f32[16,128]{1,0:T(8,128)S(1)}, u32[]{:S(2)}, u32[]{:S(2)}) collective-permute-start(f32[16,128]{1,0:T(8,128)S(1)} %multiply_add_fusion.3), channel_id=1, source_target_pairs={{0,20},{4,16},{8,28},{12,24},{16,4},{20,0},{24,12},{28,8},{1,21},{... | collective-permute-start | bytes 24584 | tf_op jit(solution)/shard_map/ppermute | solution.py:361
  79.8 4.0 %collective-permute-start.16 = (f32[16,128]{1,0:T(8,128)S(1)}, f32[16,128]{1,0:T(8,128)S(1)}, u32[]{:S(2)}, u32[]{:S(2)}) collective-permute-start(f32[16,128]{1,0:T(8,128)S(1)} %multiply_add_fusion.3), channel_id=1, source_target_pairs={{0,12},{4,8},{8,4},{12,0},{16,28},{20,24},{24,20},{28,16},{1,13},{... | collective-permute-start | bytes 24584 | tf_op jit(solution)/shard_map/ppermute | solution.py:361
  85.0 4.6 %collective-permute-start.17 = (f32[16,128]{1,0:T(8,128)S(1)}, f32[16,128]{1,0:T(8,128)S(1)}, u32[]{:S(2)}, u32[]{:S(2)}) collective-permute-start(f32[16,128]{1,0:T(8,128)S(1)} %get-tuple-element.51), channel_id=1, source_target_pairs={{0,3},{1,2},{2,1},{3,0},{4,7},{5,6},{6,5},{7,4},{8,11},{9,10},{10,... | collective-permute-start | bytes 24584 | tf_op jit(solution)/shard_map/ppermute | solution.py:375
  86.6 3.2 %collective-permute-start.18 = (f32[16,128]{1,0:T(8,128)S(1)}, f32[16,128]{1,0:T(8,128)S(1)}, u32[]{:S(2)}, u32[]{:S(2)}) collective-permute-start(f32[16,128]{1,0:T(8,128)S(1)} %get-tuple-element.51), channel_id=1, source_target_pairs={{0,6},{1,7},{2,4},{3,5},{4,2},{5,3},{6,0},{7,1},{8,14},{9,15},{10,... | collective-permute-start | bytes 24584 | tf_op jit(solution)/shard_map/ppermute | solution.py:375
  86.8 3.1 %collective-permute-start.19 = (f32[16,128]{1,0:T(8,128)S(1)}, f32[16,128]{1,0:T(8,128)S(1)}, u32[]{:S(2)}, u32[]{:S(2)}) collective-permute-start(f32[16,128]{1,0:T(8,128)S(1)} %get-tuple-element.51), channel_id=1, source_target_pairs={{0,5},{1,4},{2,7},{3,6},{4,1},{5,0},{6,3},{7,2},{8,13},{9,12},{10,... | collective-permute-start | bytes 24584 | tf_op jit(solution)/shard_map/ppermute | solution.py:375
  91.2 1.5 %collective-permute-start.20 = (f32[16,128]{1,0:T(8,128)S(1)}, f32[16,128]{1,0:T(8,128)S(1)}, u32[]{:S(2)}, u32[]{:S(2)}) collective-permute-start(f32[16,128]{1,0:T(8,128)S(1)} %shard_map.55), channel_id=1, source_target_pairs={{0,4},{4,0},{8,12},{12,8},{16,20},{20,16},{24,28},{28,24},{1,5},{5... | collective-permute-start | bytes 24584 | tf_op jit(solution)/shard_map/ppermute | solution.py:361
  92.7 4.9 %collective-permute-start.21 = (f32[16,128]{1,0:T(8,128)S(1)}, f32[16,128]{1,0:T(8,128)S(1)}, u32[]{:S(2)}, u32[]{:S(2)}) collective-permute-start(f32[16,128]{1,0:T(8,128)S(1)} %add.148), channel_id=1, source_target_pairs={{0,28},{4,24},{8,20},{12,16},{16,12},{20,8},{24,4},{28,0},{1,29},{... | collective-permute-start | bytes 24584 | tf_op jit(solution)/shard_map/ppermute | solution.py:361
  94.7 4.0 %collective-permute-start.22 = (f32[16,128]{1,0:T(8,128)S(1)}, f32[16,128]{1,0:T(8,128)S(1)}, u32[]{:S(2)}, u32[]{:S(2)}) collective-permute-start(f32[16,128]{1,0:T(8,128)S(1)} %add.148), channel_id=1, source_target_pairs={{0,20},{4,16},{8,28},{12,24},{16,4},{20,0},{24,12},{28,8},{1,21},{... | collective-permute-start | bytes 24584 | tf_op jit(solution)/shard_map/ppermute | solution.py:361
  95.4 3.4 %collective-permute-start.23 = (f32[16,128]{1,0:T(8,128)S(1)}, f32[16,128]{1,0:T(8,128)S(1)}, u32[]{:S(2)}, u32[]{:S(2)}) collective-permute-start(f32[16,128]{1,0:T(8,128)S(1)} %add.148), channel_id=1, source_target_pairs={{0,12},{4,8},{8,4},{12,0},{16,28},{20,24},{24,20},{28,16},{1,13},{... | collective-permute-start | bytes 24584 | tf_op jit(solution)/shard_map/ppermute | solution.py:361
  99.9 4.6 %collective-permute-start.24 = (f32[16,128]{1,0:T(8,128)S(1)}, f32[16,128]{1,0:T(8,128)S(1)}, u32[]{:S(2)}, u32[]{:S(2)}) collective-permute-start(f32[16,128]{1,0:T(8,128)S(1)} %shard_map.56), channel_id=1, source_target_pairs={{0,3},{1,2},{2,1},{3,0},{4,7},{5,6},{6,5},{7,4},{8,11},{9,10},{10,... | collective-permute-start | bytes 24584 | tf_op jit(solution)/shard_map/ppermute | solution.py:375
  102.3 3.1 %collective-permute-start.25 = (f32[16,128]{1,0:T(8,128)S(1)}, f32[16,128]{1,0:T(8,128)S(1)}, u32[]{:S(2)}, u32[]{:S(2)}) collective-permute-start(f32[16,128]{1,0:T(8,128)S(1)} %shard_map.56), channel_id=1, source_target_pairs={{0,6},{1,7},{2,4},{3,5},{4,2},{5,3},{6,0},{7,1},{8,14},{9,15},{10,... | collective-permute-start | bytes 24584 | tf_op jit(solution)/shard_map/ppermute | solution.py:375
  102.3 3.1 %collective-permute-start.26 = (f32[16,128]{1,0:T(8,128)S(1)}, f32[16,128]{1,0:T(8,128)S(1)}, u32[]{:S(2)}, u32[]{:S(2)}) collective-permute-start(f32[16,128]{1,0:T(8,128)S(1)} %shard_map.56), channel_id=1, source_target_pairs={{0,5},{1,4},{2,7},{3,6},{4,1},{5,0},{6,3},{7,2},{8,13},{9,12},{10,... | collective-permute-start | bytes 24584 | tf_op jit(solution)/shard_map/ppermute | solution.py:375
  106.8 1.4 %collective-permute-start.27 = (f32[16,128]{1,0:T(8,128)S(1)}, f32[16,128]{1,0:T(8,128)S(1)}, u32[]{:S(2)}, u32[]{:S(2)}) collective-permute-start(f32[16,128]{1,0:T(8,128)S(1)} %shard_map.57), channel_id=1, source_target_pairs={{0,4},{4,0},{8,12},{12,8},{16,20},{20,16},{24,28},{28,24},{1,5},{5... | collective-permute-start | bytes 24584 | tf_op jit(solution)/shard_map/ppermute | solution.py:361
  108.2 4.9 %collective-permute-start.28 = (f32[16,128]{1,0:T(8,128)S(1)}, f32[16,128]{1,0:T(8,128)S(1)}, u32[]{:S(2)}, u32[]{:S(2)}) collective-permute-start(f32[16,128]{1,0:T(8,128)S(1)} %add.155), channel_id=1, source_target_pairs={{0,28},{4,24},{8,20},{12,16},{16,12},{20,8},{24,4},{28,0},{1,29},{... | collective-permute-start | bytes 24584 | tf_op jit(solution)/shard_map/ppermute | solution.py:361
  109.8 4.0 %collective-permute-start.29 = (f32[16,128]{1,0:T(8,128)S(1)}, f32[16,128]{1,0:T(8,128)S(1)}, u32[]{:S(2)}, u32[]{:S(2)}) collective-permute-start(f32[16,128]{1,0:T(8,128)S(1)} %add.155), channel_id=1, source_target_pairs={{0,20},{4,16},{8,28},{12,24},{16,4},{20,0},{24,12},{28,8},{1,21},{... | collective-permute-start | bytes 24584 | tf_op jit(solution)/shard_map/ppermute | solution.py:361
  110.5 3.3 %collective-permute-start.30 = (f32[16,128]{1,0:T(8,128)S(1)}, f32[16,128]{1,0:T(8,128)S(1)}, u32[]{:S(2)}, u32[]{:S(2)}) collective-permute-start(f32[16,128]{1,0:T(8,128)S(1)} %add.155), channel_id=1, source_target_pairs={{0,12},{4,8},{8,4},{12,0},{16,28},{20,24},{24,20},{28,16},{1,13},{... | collective-permute-start | bytes 24584 | tf_op jit(solution)/shard_map/ppermute | solution.py:361
  113.8 15.5 %copy-start = (f32[2048]{0:T(1024)S(1)}, f32[2048]{0:T(1024)}, u32[]{:S(2)}) copy-start(f32[2048]{0:T(1024)} %param.5) | copy-start | bytes 24580
  115.0 4.6 %collective-permute-start.31 = (f32[16,128]{1,0:T(8,128)S(1)}, f32[16,128]{1,0:T(8,128)S(1)}, u32[]{:S(2)}, u32[]{:S(2)}) collective-permute-start(f32[16,128]{1,0:T(8,128)S(1)} %shard_map.58), channel_id=1, source_target_pairs={{0,3},{1,2},{2,1},{3,0},{4,7},{5,6},{6,5},{7,4},{8,11},{9,10},{10,... | collective-permute-start | bytes 24584 | tf_op jit(solution)/shard_map/ppermute | solution.py:375
  116.6 3.2 %collective-permute-start.32 = (f32[16,128]{1,0:T(8,128)S(1)}, f32[16,128]{1,0:T(8,128)S(1)}, u32[]{:S(2)}, u32[]{:S(2)}) collective-permute-start(f32[16,128]{1,0:T(8,128)S(1)} %shard_map.58), channel_id=1, source_target_pairs={{0,6},{1,7},{2,4},{3,5},{4,2},{5,3},{6,0},{7,1},{8,14},{9,15},{10,... | collective-permute-start | bytes 24584 | tf_op jit(solution)/shard_map/ppermute | solution.py:375
  116.8 3.1 %collective-permute-start.33 = (f32[16,128]{1,0:T(8,128)S(1)}, f32[16,128]{1,0:T(8,128)S(1)}, u32[]{:S(2)}, u32[]{:S(2)}) collective-permute-start(f32[16,128]{1,0:T(8,128)S(1)} %shard_map.58), channel_id=1, source_target_pairs={{0,5},{1,4},{2,7},{3,6},{4,1},{5,0},{6,3},{7,2},{8,13},{9,12},{10,... | collective-permute-start | bytes 24584 | tf_op jit(solution)/shard_map/ppermute | solution.py:375
  119.9 2.0 %collective-permute-start.34 = (f32[16,128]{1,0:T(8,128)S(1)}, f32[16,128]{1,0:T(8,128)S(1)}, u32[]{:S(2)}, u32[]{:S(2)}) collective-permute-start(f32[16,128]{1,0:T(8,128)S(1)} %get-tuple-element.54), channel_id=1, source_target_pairs={{0,4},{4,0},{8,12},{12,8},{16,20},{20,16},{24,28},{28,24},{1,5},{5... | collective-permute-start | bytes 24584 | tf_op jit(solution)/shard_map/ppermute | solution.py:361
  121.9 1.2 collective-permute-start.35
  123.1 4.9 %collective-permute-start.36 = (f32[16,128]{1,0:T(8,128)S(1)}, f32[16,128]{1,0:T(8,128)S(1)}, u32[]{:S(2)}, u32[]{:S(2)}) collective-permute-start(f32[16,128]{1,0:T(8,128)S(1)} %add.164), channel_id=1, source_target_pairs={{0,28},{4,24},{8,20},{12,16},{16,12},{20,8},{24,4},{28,0},{1,29},{... | collective-permute-start | bytes 24584 | tf_op jit(solution)/shard_map/ppermute | solution.py:361
  125.0 4.0 %collective-permute-start.37 = (f32[16,128]{1,0:T(8,128)S(1)}, f32[16,128]{1,0:T(8,128)S(1)}, u32[]{:S(2)}, u32[]{:S(2)}) collective-permute-start(f32[16,128]{1,0:T(8,128)S(1)} %add.164), channel_id=1, source_target_pairs={{0,20},{4,16},{8,28},{12,24},{16,4},{20,0},{24,12},{28,8},{1,21},{... | collective-permute-start | bytes 24584 | tf_op jit(solution)/shard_map/ppermute | solution.py:361
  125.8 3.2 %collective-permute-start.38 = (f32[16,128]{1,0:T(8,128)S(1)}, f32[16,128]{1,0:T(8,128)S(1)}, u32[]{:S(2)}, u32[]{:S(2)}) collective-permute-start(f32[16,128]{1,0:T(8,128)S(1)} %add.164), channel_id=1, source_target_pairs={{0,12},{4,8},{8,4},{12,0},{16,28},{20,24},{24,20},{28,16},{1,13},{... | collective-permute-start | bytes 24584 | tf_op jit(solution)/shard_map/ppermute | solution.py:361
